TPU v7x, 32 devices: a whole 2x2x4 slice. The times are simulated.
32 devices in a mesh: dp: 16 (over z, y, core), tensor: 2 (over x).
Axes of the slice: x: 2, y: 2, z: 4, core: 2. Of those that a mesh axis runs over, the one named last changes fastest.
Arguments:
- tokens: bfloat16 [32768, 768], P('dp'), may hold values from -6 to 6
- lengths: int32 [16, 8], P('dp'), may hold values from 1 to 1344, 1792 in all within a row
- qkv_weight: bfloat16 [3, 768, 768], P(None, None, 'tensor'), may hold values from -0.21875 to 0.21875
- qkv_bias: bfloat16 [2, 768], P(None, 'tensor'), may hold values from -3 to 3
- out_weight: bfloat16 [768, 768], P('tensor'), may hold values from -1.75 to 1.75
- out_bias: bfloat16 [768], replicated, may hold values from -3 to 3
- up_weight: bfloat16 [768, 3072], P(None, 'tensor'), may hold values from -0.21875 to 0.21875
- up_bias: bfloat16 [3072], P('tensor'), may hold values from -3 to 3
- down_weight: bfloat16 [3072, 768], P('tensor'), may hold values from -0.109375 to 0.109375
- down_bias: bfloat16 [768], replicated, may hold values from -3 to 3
- norm_gains: float32 [2, 768], replicated, may hold values from 0.5 to 1.5
- norm_biases: float32 [2, 768], replicated, may hold values from -2 to 2
- cotangent: bfloat16 [32768, 768], P('dp'), may hold values from -6 to 6
Outputs:
- output: bfloat16 [32768, 768], P('dp')
- input_grad: bfloat16 [32768, 768], P('dp')
- grad_qkv_weight: float32 [3, 768, 768], P(None, None, 'tensor')
- grad_qkv_bias: float32 [2, 768], P(None, 'tensor')
- grad_out_weight: float32 [768, 768], P('tensor')
- grad_out_bias: float32 [768], replicated
- grad_up_weight: float32 [768, 3072], P(None, 'tensor')
- grad_up_bias: float32 [3072], P('tensor')
- grad_down_weight: float32 [3072, 768], P('tensor')
- grad_down_bias: float32 [768], replicated
- grad_norm_gains: float32 [2, 768], replicated
- grad_norm_biases: float32 [2, 768], replicated
Inputs may be any that keep to these rules, and one draw needn't show every extreme that they name: Each row's lengths sum to 1792, one of them is exactly 1344; the last 256 tokens of each row are padding.
All inputs are finite; a program needn't handle non-finite values.
Results may differ from a plain program's by a relative error of at most 0.0072.
Values sent between devices are 32-bit elements; how exact they have to be, the bound alone decides.
A program may use at most 256 MiB of HBM per device.

v0:
```python
import functools
import math

import jax
import jax.numpy as jnp
import numpy as np
from jax import lax
from jax.experimental import pallas as pl
from jax.experimental.pallas import tpu as pltpu
from jax.sharding import PartitionSpec as P

HEAD = 64
ROT = 16
HALF = ROT // 2
epsilon = 1e-05
rot_base = 10000.0
f32 = jnp.float32
bf16 = jnp.bfloat16
NN = (((1,), (0,)), ((), ()))
NT = (((1,), (1,)), ((), ()))
TN = (((0,), (0,)), ((), ()))
TT = (((0,), (1,)), ((), ()))
VMEM_LIMIT = 60 * 2**20


def dot(a, b, dims=NN):
    return lax.dot_general(a, b, dims, preferred_element_type=f32)


MESH = pl.DeviceIdType.MESH


def bit_of(b):
    return lax.rem(lax.div(lax.axis_index("dp"), 1 << b), 2)


def partner(flip):
    if flip == "tensor":
        return {"tensor": 1 - lax.axis_index("tensor")}
    return {"dp": lax.axis_index("dp") + (1 - 2 * bit_of(flip)) * (1 << flip)}


def by_rows(rows, step):
    size = next(c for c in (96, 48, 24, 8, rows) if rows % c == 0)
    if rows == size:
        step(0, size)
    else:
        lax.fori_loop(0, rows // size, lambda j, c: (step(pl.multiple_of(j * size, 8), size), c)[1], 0)


class Sends:
    def __init__(self, *phases, at=(0,)):
        self.at = at
        self.phases = phases if isinstance(phases[0], list) else [list(phases)]
        moves = [m for phase in self.phases for m in phase]
        self.flips = [flip for _, flip in moves]
        self.inputs = [x for x, _ in moves if not isinstance(x, int)]
        shapes = []
        for x, _ in moves:
            shapes.append(shapes[x] if isinstance(x, int) else jax.ShapeDtypeStruct(x.shape, x.dtype))
        self.outputs = [(s, True) for s in shapes]
        self.scratch = [pltpu.SemaphoreType.DMA((2, len(moves)))]

    def build(self, ins, outs, scratch, _):
        sems, ins, events, j = scratch[0], list(ins), [], 0
        for phase in self.phases:
            copies = []
            for x, flip in phase:
                source = outs[x] if isinstance(x, int) else ins.pop(0)
                copies.append(
                    pltpu.make_async_remote_copy(
                        src_ref=source, dst_ref=outs[j], send_sem=sems.at[0, j], recv_sem=sems.at[1, j], device_id=partner(flip), device_id_type=MESH
                    )
                )
                j += 1

            def begin(copies=copies):
                for c in copies:
                    c.start()

            def finish(copies=copies):
                for c in copies:
                    c.wait()

            events.append((begin, finish))
        return events

    def receive(self, outs):
        self.got = list(outs)


class Held:
    def __init__(self, place, shape):
        self.place, self.shape = place, shape


class Sum:
    def __init__(self, keep, send, order, whole=False):
        self.mine, self.send = keep, send
        halved = [b for j, b in enumerate(order[:-1] if whole else order) if keep.shape[0] % (16 << j) == 0]
        way = [0] + halved
        self.steps = [(way[j], "halve", b) for j, b in enumerate(halved)] + [(way[-1], "add", None)]
        self.steps += [(b, "add", None) for b in order if b not in halved]
        self.steps += [(b, "join", b) for b in reversed(halved)]

    @property
    def done(self):
        return not self.steps

    def take(self, *at):
        steps, self.steps = self.steps[: len(at)], self.steps[len(at) :]
        return Steps(self, steps, at[: len(steps)])


class SmallSum(Sum):
    def __init__(self, x, bits):
        self.mine = self.send = x
        self.steps = [(b, "add", None) for b in range(bits)] + [("tensor", "norm", None)]


class Final:
    def __init__(self, sums, shapes, count, places):
        self.sums, self.shapes, self.count, self.places = sums, shapes, count, places
        self.at, self.flips = (0,), [0]

    @property
    def inputs(self):
        return [s.mine for s in self.sums]

    @property
    def outputs(self):
        return [(jax.ShapeDtypeStruct(s, f32), True) for s in self.shapes]

    @property
    def scratch(self):
        stage = [pltpu.VMEM(s.mine.shape, f32) for s in self.sums]
        return [pltpu.SemaphoreType.DMA((3, self.count)), pltpu.SemaphoreType.DMA((len(stage),))] + stage

    def build(self, ins, outs, scratch, _):
        put = lambda sources: self.places(sources, outs, bit_of(0))
        return [place_copies(put, ins, scratch[2:], 0, scratch[0], scratch[1])]

    def receive(self, outs):
        self.results = list(outs)


def place_copies(put, sources, held, flip, sems, load_sems):
    at = (lambda k, j: sems.at[k]) if load_sems is None else (lambda k, j: sems.at[k, j])
    there = [
        pltpu.make_async_remote_copy(
            src_ref=s, dst_ref=t, send_sem=at(0, j), recv_sem=at(1, j), device_id=partner(flip), device_id_type=MESH
        )
        for j, (s, t) in enumerate(put(sources))
    ]
    loads = [] if held is None else [
        pltpu.make_async_copy(s, h, sems.at[2] if load_sems is None else load_sems.at[j]) for j, (s, h) in enumerate(zip(sources, held))
    ]
    here = [pltpu.make_async_copy(s, t, at(2, j)) for j, (s, t) in enumerate(put(sources if held is None else held))]

    def begin():
        for c in there + (here if held is None else loads):
            c.start()

    def finish():
        for c in loads:
            c.wait()
        if held is not None:
            for c in here:
                c.start()
        for c in here + there:
            c.wait()

    return begin, finish


class Steps:
    def __init__(self, owner, steps, at):
        self.owner, self.steps, self.at = owner, steps, at
        self.flips = [s[0] for s in steps]
        self.same = owner.mine is owner.send
        reads = [k for _, k, _ in steps][0] in ("halve", "add", "norm")
        self.inputs = [owner.send] + ([owner.mine] if reads and not self.same else [])
        self.outputs, self.scratch = [], []
        rows, d = owner.send.shape
        self.places = None
        local = True
        if isinstance(owner.send, Held):
            self.places, self.inputs, local = (owner.send.place, owner.mine.place), [], False
        for n, (_, kind, _) in enumerate(steps):
            last = n == len(steps) - 1
            self.scratch.append(pltpu.SemaphoreType.DMA((3,)))
            if kind in ("halve", "add", "norm"):
                self.scratch += [pltpu.VMEM((rows, d), f32)] * (2 if local else 1)
                rows = rows // 2 if kind == "halve" else rows
                shapes = [(rows, d)] * (2 if kind == "halve" else 1)
                if last:
                    self.outputs += [(jax.ShapeDtypeStruct(s, f32), False) for s in shapes]
                local = False
            elif kind == "join":
                if local:
                    self.scratch.append(pltpu.VMEM((rows, d), f32))
                local = True
                rows *= 2
                self.outputs.append((jax.ShapeDtypeStruct((rows, d), f32), True))

    def build(self, ins, outs, scratch, kernel_scratch):
        outs, scratch = list(outs), list(scratch)
        if self.places is not None:
            ins = [kernel_scratch[p] for p in self.places]
        send = ins[0]
        mine = ins[-1]
        events = []
        in_hbm = self.places is None
        for n, (flip, kind, bit) in enumerate(self.steps):
            last = n == len(self.steps) - 1
            sems = scratch.pop(0)
            rows = send.shape[0]
            if kind in ("halve", "add", "norm"):
                got = scratch.pop(0)
                held = scratch.pop(0) if in_hbm else mine
                fresh = kept = None
                if last:
                    fresh = outs.pop(0)
                    kept = outs.pop(0) if kind == "halve" else None
                elif kind == "halve":
                    r, v = held.shape[0] // 2, bit_of(bit)
                    fresh, kept = (held.at[pl.ds(pl.multiple_of(h * r, 8), r)] for h in (1 - v, v))
                else:
                    fresh = held
                events.append(self.reduce(kind, bit, flip, send, mine, in_hbm, got, held, fresh, kept, sems))
                send, mine, in_hbm = fresh, (fresh if kept is None else kept), False
            elif kind == "join":
                target = outs.pop(0)
                held = scratch.pop(0) if in_hbm else None
                put = lambda xs, target=target, bit=bit, rows=rows: [
                    (xs[0], target.at[pl.ds(pl.multiple_of(bit_of(bit) * rows, 8), rows)])
                ]
                events.append(self.copies(put, send, held, flip, sems))
                send = mine = target
                in_hbm = True
        return events

    @staticmethod
    def copies(put, send, held, flip, sems, load_sems=None):
        return place_copies(put, [send], None if held is None else [held], flip, sems, load_sems)

    @staticmethod
    def reduce(kind, bit, flip, send, mine, in_hbm, got, held, fresh, kept, sems):
        there = pltpu.make_async_remote_copy(
            src_ref=send, dst_ref=got, send_sem=sems.at[0], recv_sem=sems.at[1], device_id=partner(flip), device_id_type=MESH
        )
        load = pltpu.make_async_copy(mine, held, sems.at[2]) if in_hbm else None

        def add_half(out, half, r):
            base = half * r

            def step(j, size):
                rows = pl.ds(pl.multiple_of(base + j, 8), size)
                out[pl.ds(j, size), :] = held[rows, :] + got[rows, :]

            by_rows(r, step)

        def begin():
            there.start()
            if load is not None:
                load.start()

        def after():
            if kind == "halve":
                add_half(kept, bit_of(bit), held.shape[0] // 2)

        def finish():
            if load is not None:
                load.wait()
            there.wait()
            if kind == "halve":
                r = held.shape[0] // 2
                v = bit_of(bit)
                add_half(fresh, 1 - v, r)
            elif kind == "norm":
                row = lax.broadcasted_iota(jnp.int32, held.shape, 0)
                fresh[...] = held[...] + jnp.where(row < 4, got[...], 0.0)
            else:

                def step(j, size):
                    rows = pl.ds(j, size)
                    fresh[rows, :] = held[rows, :] + got[rows, :]

                by_rows(held.shape[0], step)

        return begin, finish, after

    def receive(self, outs):
        outs = list(outs)
        owner = self.owner
        for n, (_, kind, _) in enumerate(self.steps):
            last = n == len(self.steps) - 1
            if kind == "join":
                owner.mine = owner.send = outs.pop(0)
            elif last:
                owner.send = outs.pop(0)
                owner.mine = outs.pop(0) if kind == "halve" else owner.send


def call(
    kernel, *, grid, in_specs, out_specs, out_shape, scalars=0, scratch=(), deps=(), rides=(), collective=None, flops=0, nbytes=0, name=None, aliases=None
):
    single = not isinstance(out_shape, (list, tuple))
    out_specs = [out_specs] if single else list(out_specs)
    out_shape = [out_shape] if single else list(out_shape)
    n_in, n_out, n_scratch = scalars + len(in_specs), len(out_shape), len(scratch)
    anywhere = pl.BlockSpec(memory_space=pl.ANY)
    ride_in = [x for r in rides for x in r.inputs]
    ride_out = [o for r in rides for o in r.outputs]
    flips = list(dict.fromkeys(f for r in rides for f in r.flips))

    def body(*refs):
        refs = list(refs)
        cut = lambda n: [refs.pop(0) for _ in range(n)]
        ins, _, sources = cut(n_in), cut(len(deps)), cut(len(ride_in))
        outs, targets, held = cut(n_out), cut(len(ride_out)), cut(n_scratch)
        at_step, at_end = {}, []
        for r in rides:
            take = lambda refs, n: [refs.pop(0) for _ in range(n)]
            events = r.build(take(sources, len(r.inputs)), take(targets, len(r.outputs)), take(refs, len(r.scratch)), held)
            for n, (begin, finish, *after) in enumerate(events):
                at_step.setdefault(r.at[n], ([], []))[0].append(begin)
                if n + 1 < len(events):
                    step = at_step.setdefault(r.at[n + 1], ([], []))
                    step[0].append(finish)
                    step[1].extend(after)
                else:
                    at_end += [finish] + after
        if rides:

            @pl.when(pl.program_id(0) == 0)
            def _():
                barrier = pltpu.get_barrier_semaphore()
                for f in flips:
                    pl.semaphore_signal(barrier, inc=1, device_id=partner(f), device_id_type=MESH)
                pl.semaphore_wait(barrier, len(flips))

        for g, acts in at_step.items():

            @pl.when(pl.program_id(0) == g)
            def _(acts=acts):
                for act in acts[0] + acts[1]:
                    act()

        kernel(*ins, *outs, *held)
        if at_end:

            @pl.when(pl.program_id(0) == pl.num_programs(0) - 1)
            def _():
                for act in at_end:
                    act()

    params = dict(vmem_limit_bytes=VMEM_LIMIT)
    if rides:
        params.update(collective_id=collective, has_side_effects=True)

    def run(*args):
        outs = pl.pallas_call(
            body,
            grid_spec=pltpu.PrefetchScalarGridSpec(
                num_scalar_prefetch=scalars,
                grid=grid,
                in_specs=list(in_specs) + [anywhere] * (len(deps) + len(ride_in)),
                out_specs=out_specs + [anywhere if hbm else once(s.shape) for s, hbm in ride_out],
                scratch_shapes=list(scratch) + [s for r in rides for s in r.scratch],
            ),
            out_shape=out_shape + [s for s, _ in ride_out],
            compiler_params=pltpu.CompilerParams(**params),
            cost_estimate=pl.CostEstimate(flops=20 * flops, bytes_accessed=nbytes, transcendentals=0),
            input_output_aliases=aliases or {},
            name=name,
        )(*args, *deps, *ride_in)
        outs = list(outs)
        own, rest = outs[:n_out], outs[n_out:]
        for r in rides:
            r.receive(rest[: len(r.outputs)])
            rest = rest[len(r.outputs) :]
        return own[0] if single else own

    return run


def whole(shape):
    zeros = (0,) * len(shape)
    return pl.BlockSpec(shape, lambda *_: zeros, pipeline_mode=pl.Buffered(1))


def once(shape):
    zeros = (0,) * len(shape)
    return pl.BlockSpec(shape, lambda *_: zeros)


def hat_of(values):
    average = jnp.mean(values, axis=-1, keepdims=True)
    centered = values - average
    inverse = lax.rsqrt(jnp.mean(centered * centered, axis=-1, keepdims=True) + epsilon)
    return centered * inverse, inverse


def gelu_pair(h):
    a = jnp.abs(h) * np.float32(math.sqrt(0.5))
    t = 1.0 / (1.0 + np.float32(0.3275911) * a)
    bell = jnp.exp(-0.5 * (h * h))
    poly = np.float32(0.5 * 1.061405429) * t + np.float32(0.5 * -1.453152027)
    poly = poly * t + np.float32(0.5 * 1.421413741)
    poly = poly * t + np.float32(0.5 * -0.284496736)
    poly = poly * t + np.float32(0.5 * 0.254829592)
    tail = poly * t * bell
    phi = jnp.where(h >= 0, 1.0 - tail, tail)
    return h * phi, phi + h * bell * np.float32(1.0 / math.sqrt(2.0 * math.pi))


def add_to(ref, first, value):
    @pl.when(first)
    def _():
        ref[...] = value

    @pl.when(jnp.logical_not(first))
    def _():
        ref[...] += value


def mlp_tile(chunk, tok, g, up, upb, down, gains, biases, visit):
    hat, _ = hat_of(tok[...].astype(f32))
    gain = gains[1:2, :]
    normed = (hat * gain + biases[1:2, :]).astype(bf16)
    gt = g[...]
    d = tok.shape[1]
    up_bias = jnp.concatenate([upb[c : c + 1, :] for c in range(up.shape[1] // d)], axis=1)
    total = None
    back = None
    for c in range(up.shape[1] // chunk):
        sl = slice(c * chunk, (c + 1) * chunk)
        hidden = dot(normed, up[:, sl]) + up_bias[:, sl]
        act_grad = dot(gt, down[sl, :], NT)
        act, slope = gelu_pair(hidden)
        act = act.astype(bf16)
        hid_grad = (act_grad * slope).astype(bf16)
        p = dot(act, down[sl, :])
        e = dot(hid_grad, up[:, sl], NT)
        total = p if total is None else total + p
        back = e if back is None else back + e
        visit(sl, normed, gt, act, hid_grad)
    return hat, gt, total, back, gain


def mlp_own_kernel(tok, g, up, upb, down, gains, biases, part, share, keep_a, send_a, keep_b, send_b, small, upb_sum, dup, ddown, part_s, share_s, *early):
    i = pl.program_id(0)
    tiles = pl.num_programs(0) // 2
    chunk, t = lax.div(i, tiles), lax.rem(i, tiles)
    tile, d = tok.shape

    @pl.when(i == 0)
    def _():
        small[...] = jnp.zeros_like(small)
        upb_sum[...] = jnp.zeros_like(upb_sum)
        small[0:1, :] = jnp.zeros_like(small[0:1, :])

    @pl.when(t == 0)
    def _():
        dup[...] = jnp.zeros_like(dup)
        ddown[...] = jnp.zeros_like(ddown)

    hat, _ = hat_of(tok[...].astype(f32))
    gain = gains[1:2, :]
    normed = (hat * gain + biases[1:2, :]).astype(bf16)
    gt = g[...]
    hidden = dot(normed, up[...]) + upb[pl.ds(chunk, 1), :]
    act_grad = dot(gt, down[...], NT)
    act, slope = gelu_pair(hidden)
    act = act.astype(bf16)
    hid_grad = (act_grad * slope).astype(bf16)
    total = dot(act, down[...])
    back = dot(hid_grad, up[...], NT)
    dup[...] += dot(normed, hid_grad, TN)
    ddown[...] += dot(act, gt, TN)
    upb_sum[pl.ds(chunk, 1), :] += jnp.sum(hid_grad.astype(f32), axis=0, keepdims=True)
    small[1:2, :] += jnp.sum(back * hat, axis=0, keepdims=True)
    small[2:3, :] += jnp.sum(back, axis=0, keepdims=True)
    rows = pl.ds(pl.multiple_of(t * tile, tile), tile)

    def split(first, second, first_send, second_send):
        core = bit_of(0)
        for a, b, half in ((first, second, core), (first_send, second_send, 1 - core)):
            at = pl.ds(pl.multiple_of(half * (d // 2), d // 2), d // 2)
            a[...] = ddown[at, :]
            b[...] = dup[at, :]

    @pl.when(chunk == 0)
    def _():
        small[0:1, :] += jnp.sum(gt.astype(f32), axis=0, keepdims=True)
        part_s[rows, :] = total
        share_s[rows, :] = back

        @pl.when(t == tiles - 1)
        def _():
            split(early[0], early[2], early[1], early[3])

    @pl.when(chunk == 1)
    def _():
        part[...] = part_s[rows, :] + total
        share[...] = (share_s[rows, :] + back) * gain

        @pl.when(t == tiles - 1)
        def _():
            split(keep_a, keep_b, send_a, send_b)


EARLY = 4


def mlp_own(tok, g, up, upb, down, gains, biases, tile=512, deps=(), rides=(), collective=None):
    length, d = tok.shape
    wide = up.shape[1]
    tiles = length // tile
    rows = pl.BlockSpec((tile, d), lambda i: (lax.rem(i, tiles), 0))
    out_rows = pl.BlockSpec((tile, d), lambda i: (jnp.maximum(i - tiles, 0), 0))
    half = jax.ShapeDtypeStruct((d // 2, d), f32)
    full = jax.ShapeDtypeStruct((length, d), f32)
    eight = jax.ShapeDtypeStruct((8, d), f32)
    big = pltpu.VMEM((length, d), f32)
    return call(
        mlp_own_kernel,
        grid=(2 * tiles,),
        in_specs=[
            rows, rows, pl.BlockSpec((d, wide // 2), lambda i: (0, lax.div(i, tiles))), whole((8, d)),
            pl.BlockSpec((wide // 2, d), lambda i: (lax.div(i, tiles), 0)), whole((2, d)), whole((2, d)),
        ],
        out_specs=[out_rows, out_rows, *[once(half.shape)] * 4, once((8, d)), once((8, d))],
        out_shape=[full, full, half, half, half, half, eight, eight],
        scratch=[pltpu.VMEM((d, wide // 2), f32), pltpu.VMEM((wide // 2, d), f32), big, big] + [pltpu.VMEM(half.shape, f32)] * 4,
        flops=12 * length * d * wide,
        nbytes=4 * length * d * 4,
        deps=deps,
        rides=rides,
        collective=collective,
        name="mlp_own",
    )(tok, g, up, upb, down, gains, biases)


def mlp_other_kernel(chunk, *refs):
    pieces, refs = refs[:12], refs[12:]
    tok, g, upb, gains, biases, part_in, share_in, part, share, w, ow, up, down = refs[:13]
    loaded, sems = refs[13:25], refs[25]

    @pl.when(pl.program_id(0) == 0)
    def _():
        loads = [pltpu.make_async_copy(a, b, sems.at[n]) for n, (a, b) in enumerate(zip(pieces, loaded))]
        for c in loads:
            c.start()
        for c in loads:
            c.wait()
        unpack(loaded, w, ow, up, down)

    nothing = lambda *_: None
    _, _, total, back, gain = mlp_tile(chunk, tok, g, up, upb, down, gains, biases, nothing)
    part[...] = part_in[...] + total
    share[...] = share_in[...] + back * gain


def mlp_other(pieces, tok, g, upb, gains, biases, part, share, shapes, tile=512, chunk=768, deps=(), rides=(), collective=None):
    length, d = tok.shape
    w, ow, up, down = [x.shape for x in shapes]
    rows = pl.BlockSpec((tile, d), lambda i: (i, 0))
    full = jax.ShapeDtypeStruct((length, d), f32)
    return call(
        functools.partial(mlp_other_kernel, chunk),
        grid=(length // tile,),
        in_specs=[pl.BlockSpec(memory_space=pl.ANY)] * 12 + [rows, rows, whole((8, d)), whole((2, d)), whole((2, d)), rows, rows],
        out_specs=[rows, rows, whole(w), whole(ow)],
        out_shape=[full, full, jax.ShapeDtypeStruct(w, bf16), jax.ShapeDtypeStruct(ow, bf16)],
        scratch=[pltpu.VMEM(up, bf16), pltpu.VMEM(down, bf16)] + [pltpu.VMEM(p.shape, f32) for p in pieces] + [pltpu.SemaphoreType.DMA((12,))],
        flops=8 * length * d * up[1],
        nbytes=4 * length * d * 4,
        deps=deps,
        rides=rides,
        collective=collective,
        name="mlp_other",
    )(*pieces, tok, g, upb, gains, biases, part, share)


def first_tokens(lens, places):
    first = jnp.zeros_like(places)
    end = lens[0, 0]
    for j in range(1, lens.shape[1]):
        first = jnp.where(places >= end, end, first)
        end = end + lens[0, j]
    return jnp.where(places >= end, places, first)


def turn(block, cosine, sine, sign):
    parts = []
    for h in range(block.shape[0] // HEAD):
        r = h * HEAD
        a = block[r : r + HALF, :]
        b = block[r + HALF : r + ROT, :]
        if sign > 0:
            parts += [a * cosine - b * sine, b * cosine + a * sine]
        else:
            parts += [a * cosine + b * sine, b * cosine - a * sine]
        parts.append(block[r + ROT : r + HEAD, :])
    return jnp.concatenate(parts, axis=0)


def project_tile(t, tile, bias_row, lens, tok, g, w, bias, ow, gains, biases, freq, own, q, qt, k, kpad, vpad, vone, do, dot_t, cosine, sine):
    rows = pl.ds(pl.multiple_of(t * tile, tile), tile)
    e = ow.shape[0]
    hat, _ = hat_of(tok[rows, :].astype(f32))
    normed = (hat * gains[0:1, :] + biases[0:1, :]).astype(bf16)
    places = t * tile + lax.broadcasted_iota(jnp.int32, (1, tile), 1)
    position = (places - first_tokens(lens, places)).astype(f32)
    theta = freq[:, 0:1] * position
    c = jnp.cos(theta)
    s = jnp.sin(theta)
    cosine[:, rows] = c
    sine[:, rows] = s
    row = bias[bias_row : bias_row + 1, :]
    cols = jnp.concatenate([row[:, :e], row[:, e : 2 * e], jnp.zeros((6, e), f32)], axis=0).T
    scale = HEAD ** (-0.5)
    query = turn(dot(w[0], normed, TT) + cols[:, 0:1], c, s, 1).astype(bf16) * scale
    qt[:, rows] = query
    q[rows, :] = query.T
    key = turn(dot(w[1], normed, TT), c, s, 1).astype(bf16)
    k[rows, :] = key.T
    value = (dot(w[2], normed, TT) + cols[:, 1:2]).astype(bf16)
    zero = jnp.zeros((HEAD, tile), bf16)
    if own:
        row = lax.broadcasted_iota(jnp.int32, (VROWS - HEAD, tile), 0)
        ones = jnp.where(row == 0, 1.0, 0.0).astype(bf16)
    for h in range(e // HEAD):
        sl = slice(h * HEAD, (h + 1) * HEAD)
        at, other = (0, HEAD) if h % 2 == 0 else (HEAD, 0)
        kpad[h, at : at + HEAD, rows] = key[sl, :]
        kpad[h, other : other + HEAD, rows] = zero
        vpad[h, at : at + HEAD, rows] = value[sl, :]
        vpad[h, other : other + HEAD, rows] = zero
        if own:
            vone[h, :HEAD, rows] = value[sl, :]
            vone[h, HEAD:, rows] = ones
    grad = dot(ow[...], g[rows, :], NT).astype(bf16)
    dot_t[:, rows] = grad
    do[rows, :] = grad.T


def low_parts(x):
    high = x.astype(bf16)
    rest = x - high.astype(f32)
    mid = rest.astype(bf16)
    return [high, mid, (rest - mid.astype(f32)).astype(bf16)]


FILLED = 1792


def over_tiles(q0, tk, step, carry):
    last = lax.div(q0, tk)
    first = jnp.where(q0 >= FILLED, last, 0)
    return lax.fori_loop(first, last + 1, step, carry)


VROWS = 80


def forward_tile(q0, tq, tk, first, places, qt, k, vone, ot, qpad, acc):
    heads = qt.shape[0] // HEAD
    zero = jnp.zeros((HEAD, tq), bf16)
    for h in range(heads):
        qh = qt[h * HEAD : (h + 1) * HEAD, pl.ds(q0, tq)]
        qpad[h] = jnp.concatenate([qh, zero] if h % 2 == 0 else [zero, qh], axis=0)
    acc[...] = jnp.zeros_like(acc)

    def step(j, peaks):
        k0 = pl.multiple_of(j * tk, tk)
        rows = k0 + lax.broadcasted_iota(jnp.int32, (tk, tq), 0)
        allowed = (rows >= first) & (rows <= places)
        scores, new, raised = [], [], []
        for h in range(heads):
            pair = (h // 2) * 128
            s = dot(k[pl.ds(k0, tk), pair : pair + 128], qpad[h])
            scores.append(jnp.where(allowed, s, -1e30))
        for h in range(heads):
            new.append(jnp.maximum(peaks[h], jnp.max(scores[h], axis=0, keepdims=True)))
            raised.append(jnp.exp(scores[h] - new[h]).astype(bf16))
        for h in range(heads):
            o = dot(vone[h, :, pl.ds(k0, tk)], raised[h])
            acc[h] = acc[h] * jnp.exp(peaks[h] - new[h]) + o
        return tuple(new)

    start = tuple(jnp.full((1, tq), -1e30, f32) for _ in range(heads))
    peaks = over_tiles(q0, tk, step, start)
    logs = []
    for h in range(heads):
        total = acc[h, HEAD : HEAD + 1, :]
        ot[h * HEAD : (h + 1) * HEAD, :] = acc[h, :HEAD, :] / total
        logs.append(peaks[h] + jnp.log(total))
    logs.append(jnp.zeros((8 - heads, tq), f32))
    ot[heads * HEAD :, :] = jnp.concatenate(logs, axis=0)


def backward_tile(q0, tq, tk, first, places, q, qt, k, kpad, vpad, do, dot_t, ot, cosine, sine, grads_q, dk, dv, dq, qa, da, cs, cd):
    heads = q.shape[1] // HEAD
    rows = pl.ds(q0, tq)
    deltas = [
        jnp.sum(ot[h * HEAD : (h + 1) * HEAD, :] * dot_t[h * HEAD : (h + 1) * HEAD, rows].astype(f32), axis=0, keepdims=True)
        for h in range(heads)
    ]
    deltas.append(jnp.zeros((8 - heads, tq), f32))
    stats = low_parts(ot[heads * HEAD :, :]) + low_parts(jnp.concatenate(deltas, axis=0))
    stats.append(jnp.zeros((128 - 48, tq), bf16))
    stat_cols = jnp.concatenate(stats, axis=0).T
    for r in range(heads // 2):
        pair = slice(r * 128, r * 128 + 128)
        qa[r, :, :128] = q[rows, pair]
        qa[r, :, 128:] = stat_cols
        da[r, :, :128] = do[rows, pair]
        da[r, :, 128:] = stat_cols
    dq[...] = jnp.zeros_like(dq)

    def step(j, carry):
        k0 = pl.multiple_of(j * tk, tk)
        ks = pl.ds(k0, tk)
        cols = k0 + lax.broadcasted_iota(jnp.int32, (tq, tk), 1)
        allowed = (cols >= first) & (cols <= places)
        probs, grads = [], []
        for h in range(heads):
            s = dot(qa[h // 2], jnp.concatenate([kpad[h, :, ks], cs[h]], axis=0))
            dp = dot(da[h // 2], jnp.concatenate([vpad[h, :, ks], cd[h]], axis=0))
            p = jnp.where(allowed, jnp.exp(s), 0.0)
            probs.append(p.astype(bf16))
            grads.append((p * dp).astype(bf16))
        for h in range(heads):
            sl = slice(h * HEAD, (h + 1) * HEAD)
            pair = slice((h // 2) * 128, (h // 2) * 128 + 128)
            dv[sl, ks] += dot(dot_t[sl, rows], probs[h])
            dk[sl, ks] += dot(qt[sl, rows], grads[h])
            dq[h] += dot(grads[h], k[ks, pair])
        return carry

    over_tiles(q0, tk, step, 0)
    scale = HEAD ** (-0.5)
    lane = lax.broadcasted_iota(jnp.int32, (tq, 128), 1)
    q_parts = [
        jnp.where(lane < HEAD, dq[2 * h], dq[2 * h + 1]).T * scale for h in range(heads // 2)
    ]
    grads_q[...] = turn(jnp.concatenate(q_parts, axis=0), cosine[:, rows], sine[:, rows], -1).astype(bf16)


def attention_kernel(tk, tile, own, bias_row, lens, tok_all, g_all, w, bias, ow, gains, biases, freq, *refs):
    refs = list(refs)
    cut = lambda n: [refs.pop(0) for _ in range(n)]
    if own:
        ot, ot_send, grads_q, grads_k, grads_v, keep_o, send_o = cut(7)
    else:
        ot, grads_q, grads_k, grads_v = cut(4)
    q, qt, k, kpad, vpad, do, dot_t, cosine, sine, dk, dv, dq, qa, da, cs, cd = cut(16)
    tok, g, sems = cut(3)
    vone, qpad, acc, dow = cut(4) if own else (None, None, None, None)
    i = pl.program_id(0)
    length = tok.shape[0]
    heads, tq, _ = dq.shape
    q0 = pl.multiple_of(i * tq, tq)

    @pl.when(i == 0)
    def _():
        loads = [pltpu.make_async_copy(a, b, sems.at[n]) for n, (a, b) in enumerate(((tok_all, tok), (g_all, g)))]
        for c in loads:
            c.start()
        dk[...] = jnp.zeros_like(dk)
        dv[...] = jnp.zeros_like(dv)
        row = lax.broadcasted_iota(jnp.int32, (128, tk), 0)
        for h in range(heads):
            cs[h] = jnp.where((row < 24) & (row % 8 == h), -1.0, 0.0).astype(bf16)
            cd[h] = jnp.where((row >= 24) & (row < 48) & (row % 8 == h), -1.0, 0.0).astype(bf16)

        for c in loads:
            c.wait()

        def some(t, c):
            project_tile(t, tile, bias_row, lens, tok, g, w, bias, ow, gains, biases, freq, own, q, qt, k, kpad, vpad, vone, do, dot_t, cosine, sine)
            return c

        lax.fori_loop(0, length // tile, some, 0)

    if own:
        places = q0 + lax.broadcasted_iota(jnp.int32, (1, tq), 1)
        forward_tile(q0, tq, tk, first_tokens(lens, places), places, qt, k, vone, ot, qpad, acc)
        ot_send[...] = ot[...]
        add_to(dow, i == 0, dot(ot[: ow.shape[0], :].astype(bf16), g[pl.ds(q0, tq), :]))
    places = q0 + lax.broadcasted_iota(jnp.int32, (tq, 1), 0)
    backward_tile(
        q0, tq, tk, first_tokens(lens, places), places, q, qt, k, kpad, vpad, do, dot_t, ot, cosine, sine, grads_q, dk, dv, dq, qa, da, cs, cd
    )

    @pl.when(i == pl.num_programs(0) - 1)
    def _():
        grads_k[...] = turn(dk[...], cosine[...], sine[...], -1).astype(bf16)
        grads_v[...] = dv[...].astype(bf16)
        if own:
            r = dow.shape[0] // 2
            for ref, half in ((keep_o, bit_of(0)), (send_o, 1 - bit_of(0))):
                ref[...] = dow[pl.ds(pl.multiple_of(half * r, r), r), :]


def attention(bias_row, lens, tok, g, w, bias, ow, gains, biases, freq, ot=None, tq=256, tk=256, tile=512, deps=(), rides=(), collective=None):
    length, d = tok.shape
    e = w.shape[2]
    heads = e // HEAD
    own = ot is None
    cols = pl.BlockSpec((e, tq), lambda i, *_: (0, i))
    stat = pl.BlockSpec((e + 8, tq), lambda i, *_: (0, i))
    grad = jax.ShapeDtypeStruct((e, length), bf16)
    kept = jax.ShapeDtypeStruct((e + 8, length), f32)
    nat, tr, pad, angle = pltpu.VMEM((length, e), bf16), pltpu.VMEM((e, length), bf16), pltpu.VMEM((heads, 128, length), bf16), pltpu.VMEM((HALF, length), f32)
    scratch = [nat, tr, nat, pad, pad, nat, tr, angle, angle]
    scratch += [pltpu.VMEM((e, length), f32)] * 2 + [pltpu.VMEM((heads, tq, 128), f32)]
    scratch += [pltpu.VMEM((heads // 2, tq, 256), bf16)] * 2 + [pltpu.VMEM((heads, 128, tk), bf16)] * 2
    scratch += [pltpu.VMEM((length, d), bf16)] * 2 + [pltpu.SemaphoreType.DMA((2,))]
    if own:
        scratch += [pltpu.VMEM((heads, VROWS, length), bf16), pltpu.VMEM((heads, 128, tq), bf16), pltpu.VMEM((heads, VROWS, tq), f32), pltpu.VMEM((e, d), f32)]
    half = jax.ShapeDtypeStruct((e // 2, d), f32)
    return call(
        functools.partial(attention_kernel, tk, tile, own, bias_row),
        grid=(length // tq,),
        scalars=1,
        in_specs=[
            *[pl.BlockSpec(memory_space=pl.ANY)] * 2, whole((3, d, e)), whole((8, d)), whole((e, d)), whole((2, d)), whole((2, d)), whole((HALF, 128)),
        ] + ([] if own else [stat]),
        out_specs=([stat, stat] if own else []) + [cols, whole((e, length)), whole((e, length))] + ([whole(half.shape)] * 2 if own else []),
        out_shape=([kept, kept] if own else []) + [grad, grad, grad] + ([half, half] if own else []),
        scratch=scratch,
        flops=8 * length * length * e,
        nbytes=20 * length * e,
        deps=deps,
        rides=rides,
        collective=collective,
        name="attention",
    )(lens, tok, g, w, bias, ow, gains, biases, freq, *([] if own else [ot]))


def merge_tile(tok, gq, gk, gv, ot, w, ow, gains, biases):
    hat, inverse = hat_of(tok[...].astype(f32))
    gain = gains[0:1, :]
    back = dot(gq[...], w[0], TT) + dot(gk[...], w[1], TT) + dot(gv[...], w[2], TT)
    low = ot[...].astype(bf16)
    return hat, inverse, gain, back, dot(low, ow[...], TN)


def merge_own_kernel(tok, gq, gk, gv, ot, w, ow, gains, biases, part_in, share_in, small_in, upb_in, part, share, keep_a, send_a, keep_b, send_b, small, dw):
    i = pl.program_id(0)
    tile = tok.shape[0]
    e, d = ow.shape
    n_up = 2

    @pl.when(i == 0)
    def _():
        dw[...] = jnp.zeros_like(dw)
        small[...] = jnp.zeros_like(small)
        small[1:2, :] = small_in[1:2, :]
        small[3:4, :] = small_in[2:3, :]
        small[4:5, :] = small_in[0:1, :]
        small[5 : 5 + n_up, :] = upb_in[:n_up, :]

    hat, _, gain, back, out = merge_tile(tok, gq, gk, gv, ot, w, ow, gains, biases)
    normed = (hat * gain + biases[0:1, :]).astype(bf16)
    share[...] = share_in[...] + back * gain
    part[...] = part_in[...] + out
    dw[0] += dot(normed, gq[...], TT)
    dw[1] += dot(normed, gk[...], TT)
    dw[2] += dot(normed, gv[...], TT)
    small[0:1, :] += jnp.sum(back * hat, axis=0, keepdims=True)
    small[2:3, :] += jnp.sum(back, axis=0, keepdims=True)
    ones = jnp.ones((8, tile), bf16)
    at = 5 + n_up
    small[at : at + 1, :e] += dot(ones, gq[...], NT)[0:1]
    small[at : at + 1, e : 2 * e] += dot(ones, gv[...], NT)[0:1]

    @pl.when(i == pl.num_programs(0) - 1)
    def _():
        core = bit_of(0)
        r = d // 8
        for refs, half in (((keep_a, keep_b), core), ((send_a, send_b), 1 - core)):
            for n in range(6):
                ref, at, c, sub = refs[n // 3], n % 3 * r, n // 2, n % 2
                for s in range(2):
                    rows = pl.multiple_of(half * (d // 2) + (2 * s + sub) * r, r)
                    ref[at : at + r, s * e : (s + 1) * e] = dw[c, pl.ds(rows, r), :]


def merge_own(tok, gq, gk, gv, ot, w, ow, gains, biases, part, share, small, upb, tile=512, deps=(), rides=(), collective=None):
    length, d = tok.shape
    e = w.shape[2]
    rows = pl.BlockSpec((tile, d), lambda i: (i, 0))
    cols = pl.BlockSpec((e, tile), lambda i: (0, i))
    full = jax.ShapeDtypeStruct((length, d), f32)
    half = jax.ShapeDtypeStruct((3 * d // 8, d), f32)
    return call(
        merge_own_kernel,
        grid=(length // tile,),
        in_specs=[rows, cols, cols, cols, cols, whole((3, d, e)), whole((e, d)), whole((2, d)), whole((2, d)), rows, rows, whole((8, d)), whole((8, d))],
        out_specs=[rows, rows, *[once(half.shape)] * 4, once((8, d))],
        out_shape=[full, full, half, half, half, half, jax.ShapeDtypeStruct((8, d), f32)],
        scratch=[pltpu.VMEM((3, d, e), f32)],
        flops=16 * length * d * e,
        nbytes=24 * length * d,
        deps=deps,
        rides=rides,
        collective=collective,
        name="merge_own",
    )(tok, gq, gk, gv, ot, w, ow, gains, biases, part, share, small, upb)


def merge_other_kernel(tok, g, gq, gk, gv, ot, w, ow, gains, biases, out_bias, down_bias, part_in, share_in, output, input_grad):
    hat, inverse, gain, back, out = merge_tile(tok, gq, gk, gv, ot, w, ow, gains, biases)
    shares = share_in[...] + back * gain
    inputs = tok[...].astype(f32)
    output[...] = (inputs + (part_in[...] + out) + out_bias[...].astype(f32) + down_bias[...].astype(f32)).astype(bf16)
    input_share = inverse * (
        shares
        - jnp.mean(shares, axis=-1, keepdims=True)
        - hat * jnp.mean(shares * hat, axis=-1, keepdims=True)
    )
    input_grad[...] = (g[...].astype(f32) + input_share).astype(bf16)


def merge_other(tok, g, gq, gk, gv, ot, w, ow, gains, biases, out_bias, down_bias, part, share, tile=512, deps=(), rides=(), collective=None):
    length, d = tok.shape
    e = w.shape[2]
    rows = pl.BlockSpec((tile, d), lambda i: (i, 0))
    cols = pl.BlockSpec((e, tile), lambda i: (0, i))
    full = jax.ShapeDtypeStruct((length, d), bf16)
    return call(
        merge_other_kernel,
        grid=(length // tile,),
        in_specs=[rows, rows, cols, cols, cols, cols, whole((3, d, e)), whole((e, d)), whole((2, d)), whole((2, d)), whole((1, d)), whole((1, d)), rows, rows],
        out_specs=[rows, rows],
        out_shape=[full, full],
        flops=8 * length * d * e,
        nbytes=24 * length * d,
        deps=deps,
        rides=rides,
        collective=collective,
        name="merge_other",
    )(tok, g, gq, gk, gv, ot, w, ow, gains, biases, out_bias[None], down_bias[None], part, share)


def pack_kernel(meta, w, ow, up, down, w_far, ow_far, up_far, down_far, upb, qkvb, one, two, three, four, bias_rows):
    d = ow.shape[1]
    e = w.shape[2]

    def blocks(refs):
        w, ow, up, down = refs
        for n in range(2):
            r = down.shape[0] // 8
            for s in range(4):
                yield [down[(4 * n + s) * r : (4 * n + s + 1) * r, :]]
            r = up.shape[0] // 2
            for c in range(up.shape[1] // d):
                yield [up[n * r : (n + 1) * r, c * d : (c + 1) * d]]
            r = w.shape[1] // 4
            for c in range(3):
                yield [w[c, (2 * n + s) * r : (2 * n + s + 1) * r, :] for s in range(2)]
            r = ow.shape[0] // 2
            yield [ow[n * r : (n + 1) * r, :]]

    for refs, outs in (((w, ow, up, down), (one, two, three)), ((w_far, ow_far, up_far, down_far), (None, None, four))):
        sizes = [x.shape[0] for x in (one, two, three)]
        which, at = 0, 0
        for parts in blocks(refs):
            rows, lanes = parts[0].shape
            for j, x in enumerate(parts):
                if outs[which] is not None:
                    outs[which][at : at + rows, j * lanes : (j + 1) * lanes] = x.astype(f32)
            at += rows
            if at == sizes[which]:
                which, at = which + 1, 0
    n = upb.shape[0]
    bias_rows[...] = jnp.zeros_like(bias_rows)
    bias_rows[:n, :] = upb[...].astype(f32)
    for c in range(2):
        bias_rows[n : n + 1, c * e : (c + 1) * e] = qkvb[c : c + 1, :].astype(f32)


def pack(meta, w, ow, up, down, upb, qkvb):
    _, d, e = w.shape
    wide = up.shape[1]
    rows = (wide + (wide // d) * d + 3 * d // 2 + e) // 4
    one = wide // 8 + d // 8
    two = rows // 2 - one + wide // 32
    sizes = [one, two, rows - one - two, rows - one - two, 8]
    blocks = lambda n: [
        pl.BlockSpec((3, d // 4, e), lambda i, m: (0, m[n], 0)),
        pl.BlockSpec((e // 4, d), lambda i, m: (m[n], 0)),
        pl.BlockSpec((d // 4, wide), lambda i, m: (m[n], 0)),
        pl.BlockSpec((wide // 4, d), lambda i, m: (m[n], 0)),
    ]
    return call(
        pack_kernel,
        grid=(1,),
        scalars=1,
        in_specs=blocks(0) + blocks(1) + [whole((wide // d, d)), whole((2, e))],
        out_specs=[once((r, d)) for r in sizes],
        out_shape=[jax.ShapeDtypeStruct((r, d), f32) for r in sizes],
        name="pack",
    )(meta, w, ow, up, down, w, ow, up, down, upb.reshape(-1, d), qkvb)


def unpack(pieces, w, ow, up, down):
    d = ow.shape[1]
    e = w.shape[2]
    for n in range(4):
        core = lax.rem(bit_of(0) + n // 2, 2)
        parity = lax.rem(bit_of(1) + bit_of(2) + n % 2, 2)
        refs = pieces[3 * n : 3 * n + 3]
        place = [0, 0]

        def take(rows):
            ref, at = refs[place[0]], place[1]
            place[1] = at + rows
            if place[1] == ref.shape[0]:
                place[:] = [place[0] + 1, 0]
            return ref[at : at + rows, :].astype(bf16)

        for m in range(2):
            at_piece = (parity * 2 + core) * 2 + m
            rows = lambda r, sub=0, parts=1: pl.ds(pl.multiple_of((at_piece * parts + sub) * r, r), r)
            r = down.shape[0] // 32
            for s in range(4):
                down[rows(r, s, 4), :] = take(r)
            r = up.shape[0] // 8
            for c in range(up.shape[1] // d):
                up[rows(r), c * d : (c + 1) * d] = take(r)
            r = w.shape[1] // 16
            for c in range(3):
                x = take(r)
                for s in range(2):
                    w[c, rows(r, s, 2), :] = x[:, s * e : (s + 1) * e]
            r = ow.shape[0] // 8
            ow[rows(r), :] = take(r)


def swap(x, bit):
    n = lax.axis_size("dp")
    return lax.ppermute(x, "dp", [(i, i ^ (1 << bit)) for i in range(n)])


def across(x):
    return lax.ppermute(x, "tensor", [(0, 1), (1, 0)])


def tie(arrays, deps):
    n = len(arrays)
    anywhere = [pl.BlockSpec(memory_space=pl.ANY)] * n
    return call(
        lambda *refs: None,
        grid=(1,),
        in_specs=anywhere,
        out_specs=anywhere,
        out_shape=[jax.ShapeDtypeStruct(x.shape, x.dtype) for x in arrays],
        aliases={i: i for i in range(n)},
        deps=deps,
        name="tie",
    )(*arrays)


def down_places(d, wide):
    rows = d // 2

    def places(sources, outs, core):
        return [
            (x, outs[0].at[pl.ds(pl.multiple_of(c * d + core * rows, 8), rows)]) for c, x in enumerate(sources)
        ]

    return [(wide, d)], wide // d, places


def up_places(d, wide):
    rows = d // 2

    def places(sources, outs, core):
        to = pl.ds(pl.multiple_of(core * rows, 8), rows)
        return [(x, outs[0].at[to, pl.ds(c * d, d)]) for c, x in enumerate(sources)]

    return [(d, wide)], wide // d, places


def attn_places(d, e):
    rows = d // 8

    def places(sources, outs, core):
        pairs = []
        for n in range(6):
            source, at, c, sub = sources[n // 3], n % 3 * rows, n // 2, n % 2
            for s in range(2):
                to = pl.ds(pl.multiple_of(core * (d // 2) + (2 * s + sub) * rows, 8), rows)
                pairs.append((source.at[pl.ds(at, rows), pl.ds(s * e, e)], outs[0].at[c, to]))
        to = pl.ds(pl.multiple_of(core * (e // 2), 8), e // 2)
        pairs.append((sources[2], outs[1].at[to]))
        return pairs

    return [(3, d, e), (e, d)], 13, places


def relay(rides, collective, deps=()):
    call(
        lambda *_: None,
        grid=(1,),
        in_specs=[],
        out_specs=[],
        out_shape=[],
        deps=deps,
        rides=rides,
        collective=collective,
        name="relay",
    )()


def per_device(
    tokens, lengths, qkv_weight, qkv_bias, out_weight, out_bias, up_weight, up_bias, down_weight, down_bias, norm_gains, norm_biases, cotangent
):
    length, d = tokens.shape
    e = qkv_weight.shape[2]
    wide = up_weight.shape[1]
    bits = lax.axis_size("dp").bit_length() - 1
    me = lax.axis_index("dp")
    quarter = lambda p: (((me >> 1) ^ (me >> 2) ^ p) & 1) * 2 + (me & 1)
    meta = jnp.stack([quarter(0), quarter(1)])
    freq = np.broadcast_to((rot_base ** (-(2.0 * np.arange(HALF)) / ROT)).astype(np.float32)[:, None], (HALF, 128))
    one, two, three, far_three, own_biases = pack(
        meta, qkv_weight, out_weight, up_weight, down_weight, up_bias, qkv_bias
    )
    order = list(range(1, bits))
    crossed = [order[1], order[0]] + order[2:]
    early = [Held(EARLY + j, (d // 2, d)) for j in range(4)]
    down_1, up_1 = Sum(early[0], early[1], order), Sum(early[2], early[3], crossed)
    send = Sends((one, "tensor"), (own_biases, "tensor"), (two, "tensor"))
    part, share, keep_d, send_d, keep_u, send_u, small, upb_sum = mlp_own(
        tokens, cotangent, up_weight, own_biases, down_weight, norm_gains, norm_biases,
        rides=[send, down_1.take(4, 5), up_1.take(4, 5)], collective=1,
    )
    one, other_biases, two = send.got
    down_2, up_2 = Sum(keep_d, send_d, order), Sum(keep_u, send_u, crossed)
    send = Sends((three, "tensor"), (far_three, "tensor"), (one, 0), (two, 0))
    near = [Sends((one, 1), at=(2,)), Sends((two, 1), at=(5,))]
    ot, ot_send, gq, gk, gv, keep_o, send_o = attention(
        wide // d, lengths, tokens, cotangent, qkv_weight, own_biases, out_weight, norm_gains, norm_biases, freq,
        rides=[down_1.take(0, 1, 4), up_1.take(0, 1, 4), down_2.take(0, 1, 5, 6), up_2.take(0, 1, 5, 6), send] + near, collective=2,
    )
    three, near_three, core_one, core_two = send.got
    (near_one,), (near_two,) = near[0].got, near[1].got
    other_ot = across(ot_send)
    sum_o = Sum(keep_o, send_o, order, True)
    send = Sends((near_one, 0), (near_two, 0), (near_three, 0), (three, 0))
    part, share, keep_a, send_a, keep_b, send_b, small = merge_own(
        tokens, gq, gk, gv, ot, qkv_weight, out_weight, norm_gains, norm_biases, part, share, small, upb_sum,
        rides=[down_2.take(0), up_2.take(0), down_1.take(0), up_1.take(0), sum_o.take(0), send], collective=3,
    )
    core_near_one, core_near_two, core_near_three, core_three = send.got
    sum_a, sum_b, sum_s = Sum(keep_a, send_a, order, True), Sum(keep_b, send_b, crossed, True), SmallSum(small, bits)
    pieces = [one, two, three, near_one, near_two, near_three]
    pieces += [core_one, core_two, core_three, core_near_one, core_near_two, core_near_three]
    part, share, other_w, other_ow = mlp_other(
        pieces, tokens, cotangent, other_biases, norm_gains, norm_biases, part, share, [qkv_weight, out_weight, up_weight, down_weight],
        rides=[
            sum_s.take(0, 1), sum_a.take(0), sum_b.take(0), down_2.take(0, 1), up_2.take(0, 1), down_1.take(0), up_1.take(0),
        ],
        collective=4,
    )
    at = 7
    mlp_sums = [down_1, down_2, up_1, up_2]
    while not all(s.done for s in mlp_sums):
        relay([s.take(0) for s in mlp_sums if not s.done], at)
        at += 1
    final_d, final_u = Final(mlp_sums[:2], *down_places(d, wide)), Final(mlp_sums[2:], *up_places(d, wide))
    (other_ot,) = tie([other_ot], [part])
    gq, gk, gv = attention(
        wide // d, lengths, tokens, cotangent, other_w, other_biases, other_ow, norm_gains, norm_biases, freq, other_ot,
        rides=[sum_s.take(0, 1, 2)] + [s.take(0, 2, 4) for s in (sum_a, sum_b, sum_o)], collective=5,
    )
    sums = [sum_a, sum_b, sum_o, sum_s]
    output, input_grad = merge_other(
        tokens, cotangent, gq, gk, gv, other_ot, other_w, other_ow, norm_gains, norm_biases, out_bias, down_bias, part, share,
        rides=[s.take(0, 2) for s in sums if not s.done] + [final_d, final_u], collective=6,
    )
    while not all(s.done for s in sums):
        relay([s.take(0) for s in sums if not s.done], at)
        at += 1
    final = Final(sums[:3], *attn_places(d, e))
    relay([final], at)
    (d_down,), (d_up,), (d_qkv, d_out) = final_d.results, final_u.results, final.results
    small = sum_s.mine
    rest = small[5:].reshape(-1)
    return (
        output, input_grad, d_qkv, rest[wide : wide + 2 * e].reshape(2, e), d_out, small[4], d_up, rest[:wide], d_down, small[4], small[:2], small[2:4],
    )


def solution(mesh):
    in_specs = (
        P("dp", None), P("dp", None), P(None, None, "tensor"), P(None, "tensor"), P("tensor", None), P(), P(None, "tensor"),
        P("tensor"), P("tensor", None), P(), P(), P(), P("dp", None),
    )
    out_specs = (
        P("dp", None), P("dp", None), P(None, None, "tensor"), P(None, "tensor"), P("tensor", None), P(), P(None, "tensor"),
        P("tensor"), P("tensor", None), P(), P(), P(),
    )
    return jax.shard_map(per_device, mesh=mesh, in_specs=in_specs, out_specs=out_specs, check_vma=False)
```

profile of v0, /device:TPU:0, one launch (start us, length us, event | category | flops | bytes accessed | tf_op | source)
XLA Modules:
  0.0 339.3 jit_solution(1545239998227077384)
XLA Ops:
  0.7 1.3 reshape.34.refs_9_
  1.9 0.6 pad_add_fusion.refs_0_
  2.5 5.1 %pack.1 = (f32[288,768]{1,0:T(8,128)}, f32[336,768]{1,0:T(8,128)}, f32[528,768]{1,0:T(8,128)}, f32[528,768]{1,0:T(8,128)}, f32[8,768]{1,0:T(8,128)}) custom-call(s32[2]{0:T(128)} %pad_add_fusion.refs_0_, bf16[3,768,384]{2,1,0:T(8,128)(2,1)} %refs_5_.7, bf16[384,768]{1,0:T(8,128)(2,1)} %refs_6_.8, bf16[768,1536]{1,0:T(8,128)(2,1)} %refs_2_.5, ...), custom_call_target="tpu_custom_call" | custom-call | tf_op jit(solution)/shard_map/pack/pallas_call | solution.py:363
  7.6 0.0 copy-start.6
  7.6 54.6 %mlp_own.1 = (f32[2048,768]{1,0:T(8,128)}, f32[2048,768]{1,0:T(8,128)}, f32[384,768]{1,0:T(8,128)}, f32[384,768]{1,0:T(8,128)}, f32[384,768]{1,0:T(8,128)}, /*in...) custom-call(bf16[2048,768]{1,0:T(8,128)(2,1)} %refs_0_.9, ...), custom_call_target="tpu_custom_call" | custom-call | flops 579820584960 | bytes 25165824 | tf_op jit(solution)/shard_map/mlp_own/pallas_call | solution.py:363
  62.2 0.0 copy-done.6
  62.2 0.7 jit_solution_.3.refs_8_
  62.9 84.5 %attention.2 = (f32[392,2048]{1,0:T(8,128)}, f32[392,2048]{1,0:T(8,128)}, bf16[384,2048]{1,0:T(8,128)(2,1)}, bf16[384,2048]{1,0:T(8,128)(2,1)}, bf16[384,2048]{1...) custom-call(s32[1,8]{1,0:T(1,128)} %refs_0_.8, ...), custom_call_target="tpu_custom_call" | custom-call | flops 257698037760 | bytes 15728640 | tf_op jit(solution)/shard_map/attention/pallas_call | solution.py:363
  147.5 1.6 collective-permute-start
  149.0 26.1 %merge_own.1 = (f32[2048,768]{1,0:T(8,128)}, f32[2048,768]{1,0:T(8,128)}, f32[288,768]{1,0:T(8,128)}, f32[288,768]{1,0:T(8,128)}, f32[288,768]{1,0:T(8,128)}, /*...) custom-call(bf16[2048,768]{1,0:T(8,128)(2,1)} %refs_0_.9, ...), custom_call_target="tpu_custom_call" | custom-call | flops 193273528320 | bytes 37748736 | tf_op jit(solution)/shard_map/merge_own/pallas_call | solution.py:363
  175.1 0.0 copy-start.4
  175.1 0.0 copy-start.5
  175.1 45.2 %mlp_other.1 = (f32[2048,768]{1,0:T(8,128)}, f32[2048,768]{1,0:T(8,128)}, bf16[3,768,384]{2,1,0:T(8,128)(2,1)}, bf16[384,768]{1,0:T(8,128)(2,1)}, f32[8,768]{1,0...) custom-call(f32[288,768]{1,0:T(8,128)} %get-tuple-element.98.refs_19, ...), custom_call_target="tpu_custom_call" | custom-call | flops 386547056640 | bytes 25165824 | tf_op jit(solution)/shard_map/mlp_other/pallas_call | solution.py:363
  220.3 0.0 copy-done.4
  220.3 0.6 broadcast_in_dim.6.refs_10_
  220.9 0.0 copy-done.5
  220.9 0.6 broadcast_in_dim.7.refs_11_
  221.4 0.0 collective-permute-done.refs_0_
  221.5 58.2 %attention.3 = (bf16[384,2048]{1,0:T(8,128)(2,1)}, bf16[384,2048]{1,0:T(8,128)(2,1)}, bf16[384,2048]{1,0:T(8,128)(2,1)}, f32[8,768]{1,0:T(8,128)}, f32[72,768]{1...) custom-call(s32[1,8]{1,0:T(1,128)} %refs_0_.8, bf16[2048,768]{1,0:T(8,128)(2,1)} %refs_0_.9, ...), custom_call_target="tpu_custom_call" | custom-call | flops 257698037760 | bytes 15728640 | tf_op jit(solution)/shard_map/attention/pallas_call | solution.py:363
  279.6 1.5 fusion
  281.1 0.8 slice_reduce_fusion
  281.9 0.0 copy-start.3
  281.9 34.6 %merge_other.1 = (bf16[2048,768]{1,0:T(8,128)(2,1)}, bf16[2048,768]{1,0:T(8,128)(2,1)}, f32[144,768]{1,0:T(8,128)}, f32[288,768]{1,0:T(8,128)}, f32[144,768]{1,0...) custom-call(bf16[2048,768]{1,0:T(8,128)(2,1)} %refs_0_.9, ...), custom_call_target="tpu_custom_call" | custom-call | flops 96636764160 | bytes 37748736 | tf_op jit(solution)/shard_map/merge_other/pallas_call | solution.py:363
  316.6 0.0 copy-start.1
  316.6 5.3 %relay.1 = (f32[3,768,384]{2,1,0:T(8,128)}, f32[384,768]{1,0:T(8,128)}) custom-call(f32[288,768]{1,0:T(8,128)} %get-tuple-element.170.refs_0_, f32[288,768]{1,0:T(8,128)} %get-tuple-element.171.refs_1_, f32[192,768]{1,0:T(8,128)} %get-tuple-element.172.refs_2_), custom_call_target="tpu_custom_call" | custom-call | tf_op jit(solution)/shard_map/relay/pallas_call | solution.py:363
  321.9 0.6 slice.26
  322.5 0.6 reshape.35
  323.1 0.0 copy-done.3
  323.1 0.6 copy.35
  323.7 0.0 copy-start
  323.7 3.9 %copy.36 = bf16[2048,768]{1,0:T(8,128)(2,1)} copy(bf16[2048,768]{1,0:T(8,128)(2,1)} %get-tuple-element.219) | data formatting | bytes 6291456
  327.6 0.0 copy-done.1
  327.6 0.0 slice-start.2
  327.6 1.7 copy.37
  329.2 0.0 copy-done
  329.2 0.0 copy-start.2
  329.3 0.0 slice-start.3
  329.3 1.8 copy.38
  331.1 1.5 copy-done.2
  332.5 0.0 slice-start
  332.5 1.0 copy.39
  333.5 0.0 slice-done.2
  333.5 0.0 slice-done.3
  333.5 0.0 slice-start.1
  333.6 2.4 copy.40
  336.0 0.8 slice-done
  336.8 0.3 slice-done.1
  337.1 2.2 copy.41
  (3 shorter events, 0.0 us)
Async XLA Ops:
  7.6 54.6 %copy-start.6 = (f32[8]{0:T(128)S(1)}, f32[8]{0:T(128)}, u32[]{:S(2)}) copy-start(f32[8]{0:T(128)} %constant.12.clone) | copy-start | bytes 100
  147.5 74.0 %collective-permute-start = (f32[392,2048]{1,0:T(8,128)}, f32[392,2048]{1,0:T(8,128)}, u32[]{:S(2)}, u32[]{:S(2)}) collective-permute-start(f32[392,2048]{1,0:T(8,128)} %get-tuple-element.148), channel_id=1, source_target_pairs={{0,1},{1,0},{2,3},{3,2},{4,5},{5,4},{6,7},{7,6},{8,9},{9,8},{10,11... | collective-permute-start | bytes 9633800 | tf_op jit(solution)/shard_map/ppermute | solution.py:1052
  175.1 45.2 %copy-start.4 = (bf16[768]{0:T(1024)(128)(2,1)S(1)}, bf16[768]{0:T(1024)(128)(2,1)}, u32[]{:S(2)}) copy-start(bf16[768]{0:T(1024)(128)(2,1)} %param.19) | copy-start | bytes 4612
  175.1 45.8 %copy-start.5 = (bf16[768]{0:T(1024)(128)(2,1)S(1)}, bf16[768]{0:T(1024)(128)(2,1)}, u32[]{:S(2)}) copy-start(bf16[768]{0:T(1024)(128)(2,1)} %param.23) | copy-start | bytes 4612
  281.9 41.1 %copy-start.3 = (f32[768]{0:T(1024)}, f32[768]{0:T(1024)S(1)}, u32[]{:S(2)}) copy-start(f32[768]{0:T(1024)S(1)} %get-tuple-element.224) | copy-start | bytes 9220
  316.6 11.0 %copy-start.1 = (bf16[2048,768]{1,0:T(8,128)(2,1)S(1)}, bf16[2048,768]{1,0:T(8,128)(2,1)}, u32[]{:S(2)}) copy-start(bf16[2048,768]{1,0:T(8,128)(2,1)} %get-tuple-element.220) | copy-start | bytes 9437188
  323.7 5.6 %copy-start = (f32[3,768,384]{2,1,0:T(8,128)S(1)}, f32[3,768,384]{2,1,0:T(8,128)}, u32[]{:S(2)}) copy-start(f32[3,768,384]{2,1,0:T(8,128)} %get-tuple-element.221) | copy-start | bytes 10616836
  327.6 6.0 %slice-start.2 = ((s8[4718592]{0:T(1024)(128)(4,1)}), s8[4194304]{0:T(1024)(128)(4,1)S(1)}, s32[]{:S(2)}) async-start(s8[4718592]{0:T(1024)(128)(4,1)} %bitcast.4), calls=%async_computation.2 | async-start | bytes 8388608
  329.2 3.3 copy-start.2
  329.3 4.3 %slice-start.3 = ((s8[4718592]{0:T(1024)(128)(4,1)}), s8[524288]{0:T(1024)(128)(4,1)S(1)}, s32[]{:S(2)}) async-start(s8[4718592]{0:T(1024)(128)(4,1)} %bitcast.4), calls=%async_computation.3 | async-start | bytes 1048576
  332.5 4.3 %slice-start = ((s8[4718592]{0:T(1024)(128)(4,1)}), s8[4194304]{0:T(1024)(128)(4,1)S(1)}, s32[]{:S(2)}) async-start(s8[4718592]{0:T(1024)(128)(4,1)} %bitcast.2), calls=%async_computation | async-start | bytes 8388608
  333.5 3.5 %slice-start.1 = ((s8[4718592]{0:T(1024)(128)(4,1)}), s8[524288]{0:T(1024)(128)(4,1)S(1)}, s32[]{:S(2)}) async-start(s8[4718592]{0:T(1024)(128)(4,1)} %bitcast.2), calls=%async_computation.1 | async-start | bytes 1048576
where the time goes:
time: 340 us; the launch traced here: 339 us
  Pallas kernels  314 us (92%)
  local copies, waits for them, and re-layouts  22.8 us (7%)
    pallas_call x9, Pallas kernels, run(): pl.pallas_call(body, grid_spec=pltpu.PrefetchScalarGridSpec(num_scalar_pr...  314 us
    unnamed x29, local copies, waits for them, and re-layouts  16.2 us
  transfers between devices with their start and end apart: 1, of which 0 were waited for; matrix products, arithmetic and copies ran while one was open for 0% of the time, Pallas kernels for 21%

commit v1 on v0

--- a/solution.py
+++ b/solution.py
@@ -413,16 +413,6 @@
     tail = poly * t * bell
     phi = jnp.where(h >= 0, 1.0 - tail, tail)
     return h * phi, phi + h * bell * np.float32(1.0 / math.sqrt(2.0 * math.pi))
-
-
-def add_to(ref, first, value):
-    @pl.when(first)
-    def _():
-        ref[...] = value
-
-    @pl.when(jnp.logical_not(first))
-    def _():
-        ref[...] += value
 
 
 def mlp_tile(chunk, tok, g, up, upb, down, gains, biases, visit):
@@ -759,7 +749,7 @@
         ot, grads_q, grads_k, grads_v = cut(4)
     q, qt, k, kpad, vpad, do, dot_t, cosine, sine, dk, dv, dq, qa, da, cs, cd = cut(16)
     tok, g, sems = cut(3)
-    vone, qpad, acc, dow = cut(4) if own else (None, None, None, None)
+    vone, qpad, acc, dow, low = cut(5) if own else (None, None, None, None, None)
     i = pl.program_id(0)
     length = tok.shape[0]
     heads, tq, _ = dq.shape
@@ -790,7 +780,7 @@
         places = q0 + lax.broadcasted_iota(jnp.int32, (1, tq), 1)
         forward_tile(q0, tq, tk, first_tokens(lens, places), places, qt, k, vone, ot, qpad, acc)
         ot_send[...] = ot[...]
-        add_to(dow, i == 0, dot(ot[: ow.shape[0], :].astype(bf16), g[pl.ds(q0, tq), :]))
+        low[:, pl.ds(q0, tq)] = ot[: ow.shape[0], :].astype(bf16)
     places = q0 + lax.broadcasted_iota(jnp.int32, (tq, 1), 0)
     backward_tile(
         q0, tq, tk, first_tokens(lens, places), places, q, qt, k, kpad, vpad, do, dot_t, ot, cosine, sine, grads_q, dk, dv, dq, qa, da, cs, cd
@@ -801,6 +791,7 @@
         grads_k[...] = turn(dk[...], cosine[...], sine[...], -1).astype(bf16)
         grads_v[...] = dv[...].astype(bf16)
         if own:
+            dow[...] = dot(low[...], g[...])
             r = dow.shape[0] // 2
             for ref, half in ((keep_o, bit_of(0)), (send_o, 1 - bit_of(0))):
                 ref[...] = dow[pl.ds(pl.multiple_of(half * r, r), r), :]
@@ -821,7 +812,7 @@
     scratch += [pltpu.VMEM((heads // 2, tq, 256), bf16)] * 2 + [pltpu.VMEM((heads, 128, tk), bf16)] * 2
     scratch += [pltpu.VMEM((length, d), bf16)] * 2 + [pltpu.SemaphoreType.DMA((2,))]
     if own:
-        scratch += [pltpu.VMEM((heads, VROWS, length), bf16), pltpu.VMEM((heads, 128, tq), bf16), pltpu.VMEM((heads, VROWS, tq), f32), pltpu.VMEM((e, d), f32)]
+        scratch += [pltpu.VMEM((heads, VROWS, length), bf16), pltpu.VMEM((heads, 128, tq), bf16), pltpu.VMEM((heads, VROWS, tq), f32), pltpu.VMEM((e, d), f32), tr]
     half = jax.ShapeDtypeStruct((e // 2, d), f32)
     return call(
         functools.partial(attention_kernel, tk, tile, own, bias_row),
@@ -1166,31 +1157,29 @@
     part, share, other_w, other_ow = mlp_other(
         pieces, tokens, cotangent, other_biases, norm_gains, norm_biases, part, share, [qkv_weight, out_weight, up_weight, down_weight],
         rides=[
-            sum_s.take(0, 1), sum_a.take(0), sum_b.take(0), down_2.take(0, 1), up_2.take(0, 1), down_1.take(0), up_1.take(0),
+            sum_s.take(0, 3), sum_a.take(0, 1, 3), sum_b.take(0, 1, 3), sum_o.take(1, 3), down_2.take(0), up_2.take(0), down_1.take(0), up_1.take(0),
         ],
         collective=4,
     )
-    at = 7
-    mlp_sums = [down_1, down_2, up_1, up_2]
-    while not all(s.done for s in mlp_sums):
-        relay([s.take(0) for s in mlp_sums if not s.done], at)
-        at += 1
-    final_d, final_u = Final(mlp_sums[:2], *down_places(d, wide)), Final(mlp_sums[2:], *up_places(d, wide))
     (other_ot,) = tie([other_ot], [part])
     gq, gk, gv = attention(
         wide // d, lengths, tokens, cotangent, other_w, other_biases, other_ow, norm_gains, norm_biases, freq, other_ot,
-        rides=[sum_s.take(0, 1, 2)] + [s.take(0, 2, 4) for s in (sum_a, sum_b, sum_o)], collective=5,
+        rides=[s.take(0, 5, 6) for s in (sum_a, sum_b, sum_o)] + [down_2.take(0), up_2.take(0), sum_s.take(0, 6)], collective=5,
     )
-    sums = [sum_a, sum_b, sum_o, sum_s]
-    output, input_grad = merge_other(
-        tokens, cotangent, gq, gk, gv, other_ot, other_w, other_ow, norm_gains, norm_biases, out_bias, down_bias, part, share,
-        rides=[s.take(0, 2) for s in sums if not s.done] + [final_d, final_u], collective=6,
-    )
+    at = 7
+    sums = [down_1, down_2, up_1, up_2, sum_a, sum_b, sum_o]
     while not all(s.done for s in sums):
         relay([s.take(0) for s in sums if not s.done], at)
         at += 1
-    final = Final(sums[:3], *attn_places(d, e))
-    relay([final], at)
+    final_d, final_u = Final(sums[:2], *down_places(d, wide)), Final(sums[2:4], *up_places(d, wide))
+    final = Final(sums[4:], *attn_places(d, e))
+    output, input_grad = merge_other(
+        tokens, cotangent, gq, gk, gv, other_ot, other_w, other_ow, norm_gains, norm_biases, out_bias, down_bias, part, share,
+        rides=[sum_s.take(0), final_d, final_u, final], collective=6,
+    )
+    while not sum_s.done:
+        relay([sum_s.take(0)], at)
+        at += 1
     (d_down,), (d_up,), (d_qkv, d_out) = final_d.results, final_u.results, final.results
     small = sum_s.mine
     rest = small[5:].reshape(-1)

time: 340 us -> 334 us (0.982)
  Pallas kernels: 314 us -> 308 us
    pallas_call x9 -> x8, Pallas kernels: 314 us -> 308 us  [run(): pl.pallas_call(body, grid_spec=pltpu.PrefetchScalarGridSpec(num_scalar_pr...]
  transfers between devices with their start and end apart: 1 -> 1, of which waited for: 0 -> 0; matrix products, arithmetic and copies ran while one was open for 0% -> 0% of each run, Pallas kernels for 21% -> 24%
where the time goes in v1:
time: 334 us; the launch traced here: 333 us
  Pallas kernels  308 us (92%)
  local copies, waits for them, and re-layouts  22.9 us (7%)
    pallas_call x8, Pallas kernels, run(): pl.pallas_call(body, grid_spec=pltpu.PrefetchScalarGridSpec(num_scalar_pr...  308 us
    unnamed x29, local copies, waits for them, and re-layouts  16.2 us
  transfers between devices with their start and end apart: 1, of which 0 were waited for; matrix products, arithmetic and copies ran while one was open for 0% of the time, Pallas kernels for 24%

profile of v1, /device:TPU:0, one launch (start us, length us, event | category | flops | bytes accessed | tf_op | source)
XLA Modules:
  0.0 333.3 jit_solution(5310278139235497053)
XLA Ops:
  0.7 1.3 reshape.34.refs_9_
  1.9 0.6 pad_add_fusion.refs_0_
  2.5 5.1 %pack.1 = (f32[288,768]{1,0:T(8,128)}, f32[336,768]{1,0:T(8,128)}, f32[528,768]{1,0:T(8,128)}, f32[528,768]{1,0:T(8,128)}, f32[8,768]{1,0:T(8,128)}) custom-call(s32[2]{0:T(128)} %pad_add_fusion.refs_0_, bf16[3,768,384]{2,1,0:T(8,128)(2,1)} %refs_5_.7, bf16[384,768]{1,0:T(8,128)(2,1)} %refs_6_.8, bf16[768,1536]{1,0:T(8,128)(2,1)} %refs_2_.5, ...), custom_call_target="tpu_custom_call" | custom-call | tf_op jit(solution)/shard_map/pack/pallas_call | solution.py:363
  7.6 0.0 copy-start.6
  7.6 54.7 %mlp_own.1 = (f32[2048,768]{1,0:T(8,128)}, f32[2048,768]{1,0:T(8,128)}, f32[384,768]{1,0:T(8,128)}, f32[384,768]{1,0:T(8,128)}, f32[384,768]{1,0:T(8,128)}, /*in...) custom-call(bf16[2048,768]{1,0:T(8,128)(2,1)} %refs_0_.9, ...), custom_call_target="tpu_custom_call" | custom-call | flops 579820584960 | bytes 25165824 | tf_op jit(solution)/shard_map/mlp_own/pallas_call | solution.py:363
  62.3 0.0 copy-done.6
  62.3 0.7 jit_solution_.3.refs_8_
  63.0 84.2 %attention.2 = (f32[392,2048]{1,0:T(8,128)}, f32[392,2048]{1,0:T(8,128)}, bf16[384,2048]{1,0:T(8,128)(2,1)}, bf16[384,2048]{1,0:T(8,128)(2,1)}, bf16[384,2048]{1...) custom-call(s32[1,8]{1,0:T(1,128)} %refs_0_.8, ...), custom_call_target="tpu_custom_call" | custom-call | flops 257698037760 | bytes 15728640 | tf_op jit(solution)/shard_map/attention/pallas_call | solution.py:363
  147.2 1.6 collective-permute-start
  148.8 26.2 %merge_own.1 = (f32[2048,768]{1,0:T(8,128)}, f32[2048,768]{1,0:T(8,128)}, f32[288,768]{1,0:T(8,128)}, f32[288,768]{1,0:T(8,128)}, f32[288,768]{1,0:T(8,128)}, /*...) custom-call(bf16[2048,768]{1,0:T(8,128)(2,1)} %refs_0_.9, ...), custom_call_target="tpu_custom_call" | custom-call | flops 193273528320 | bytes 37748736 | tf_op jit(solution)/shard_map/merge_own/pallas_call | solution.py:363
  174.9 0.0 copy-start.4
  174.9 0.0 copy-start.5
  175.0 53.9 %mlp_other.1 = (f32[2048,768]{1,0:T(8,128)}, f32[2048,768]{1,0:T(8,128)}, bf16[3,768,384]{2,1,0:T(8,128)(2,1)}, bf16[384,768]{1,0:T(8,128)(2,1)}, f32[8,768]{1,0...) custom-call(f32[288,768]{1,0:T(8,128)} %get-tuple-element.97.refs_19, ...), custom_call_target="tpu_custom_call" | custom-call | flops 386547056640 | bytes 25165824 | tf_op jit(solution)/shard_map/mlp_other/pallas_call | solution.py:363
  228.9 0.0 copy-done.4
  228.9 0.6 broadcast_in_dim.6.refs_10_
  229.5 0.0 copy-done.5
  229.5 0.6 broadcast_in_dim.7.refs_11_
  230.1 0.0 collective-permute-done.refs_0_
  230.1 61.2 %attention.3 = (bf16[384,2048]{1,0:T(8,128)(2,1)}, bf16[384,2048]{1,0:T(8,128)(2,1)}, bf16[384,2048]{1,0:T(8,128)(2,1)}, f32[144,768]{1,0:T(8,128)}, f32[288,768...) custom-call(s32[1,8]{1,0:T(1,128)} %refs_0_.8, ...), custom_call_target="tpu_custom_call" | custom-call | flops 257698037760 | bytes 15728640 | tf_op jit(solution)/shard_map/attention/pallas_call | solution.py:363
  291.3 22.3 %merge_other.1 = (bf16[2048,768]{1,0:T(8,128)(2,1)}, bf16[2048,768]{1,0:T(8,128)(2,1)}, f32[8,768]{1,0:T(8,128)}, f32[1536,768]{1,0:T(8,128)}, f32[768,1536]{1,0...) custom-call(bf16[2048,768]{1,0:T(8,128)(2,1)} %refs_0_.9, bf16[2048,768]{1,0:T(8,128)(2,1)} %refs_1_.9, ...), custom_call_target="tpu_custom_call" | custom-call | flops 96636764160 | bytes 37748736 | tf_op jit(solution)/shard_map/merge_other/pallas_call | solution.py:363
  313.6 1.5 fusion
  315.0 0.0 copy-start.1
  315.0 0.9 slice_reduce_fusion
  315.9 0.0 copy-start.3
  315.9 0.6 slice.26
  316.6 0.6 reshape.35
  317.1 0.6 copy.35
  317.7 0.0 copy-start
  317.7 3.9 %copy.36 = bf16[2048,768]{1,0:T(8,128)(2,1)} copy(bf16[2048,768]{1,0:T(8,128)(2,1)} %get-tuple-element.217) | data formatting | bytes 6291456
  321.6 0.0 copy-done.3
  321.6 0.0 copy-done.1
  321.6 0.0 slice-start.2
  321.7 1.7 copy.37
  323.3 0.0 copy-done
  323.3 0.0 copy-start.2
  323.3 0.0 slice-start.3
  323.3 1.8 copy.38
  325.1 1.5 copy-done.2
  326.6 0.0 slice-start
  326.6 1.0 copy.39
  327.6 0.0 slice-done.2
  327.6 0.0 slice-done.3
  327.6 0.0 slice-start.1
  327.6 2.4 copy.40
  330.0 0.8 slice-done
  330.9 0.3 slice-done.1
  331.2 2.2 copy.41
  (3 shorter events, 0.0 us)
Async XLA Ops:
  7.6 54.7 %copy-start.6 = (f32[8]{0:T(128)S(1)}, f32[8]{0:T(128)}, u32[]{:S(2)}) copy-start(f32[8]{0:T(128)} %constant.12.clone) | copy-start | bytes 100
  147.2 82.9 %collective-permute-start = (f32[392,2048]{1,0:T(8,128)}, f32[392,2048]{1,0:T(8,128)}, u32[]{:S(2)}, u32[]{:S(2)}) collective-permute-start(f32[392,2048]{1,0:T(8,128)} %get-tuple-element.149), channel_id=1, source_target_pairs={{0,1},{1,0},{2,3},{3,2},{4,5},{5,4},{6,7},{7,6},{8,9},{9,8},{10,11... | collective-permute-start | bytes 9633800 | tf_op jit(solution)/shard_map/ppermute | solution.py:1043
  174.9 54.0 %copy-start.4 = (bf16[768]{0:T(1024)(128)(2,1)S(1)}, bf16[768]{0:T(1024)(128)(2,1)}, u32[]{:S(2)}) copy-start(bf16[768]{0:T(1024)(128)(2,1)} %param.19) | copy-start | bytes 4612
  174.9 54.6 %copy-start.5 = (bf16[768]{0:T(1024)(128)(2,1)S(1)}, bf16[768]{0:T(1024)(128)(2,1)}, u32[]{:S(2)}) copy-start(bf16[768]{0:T(1024)(128)(2,1)} %param.23) | copy-start | bytes 4612
  315.0 6.6 %copy-start.1 = (bf16[2048,768]{1,0:T(8,128)(2,1)S(1)}, bf16[2048,768]{1,0:T(8,128)(2,1)}, u32[]{:S(2)}) copy-start(bf16[2048,768]{1,0:T(8,128)(2,1)} %get-tuple-element.218) | copy-start | bytes 9437188
  315.9 5.7 %copy-start.3 = (f32[768]{0:T(1024)}, f32[768]{0:T(1024)S(1)}, u32[]{:S(2)}) copy-start(f32[768]{0:T(1024)S(1)} %get-tuple-element.222) | copy-start | bytes 9220
  317.7 5.6 %copy-start = (f32[3,768,384]{2,1,0:T(8,128)S(1)}, f32[3,768,384]{2,1,0:T(8,128)}, u32[]{:S(2)}) copy-start(f32[3,768,384]{2,1,0:T(8,128)} %get-tuple-element.219) | copy-start | bytes 10616836
  321.6 6.0 %slice-start.2 = ((s8[4718592]{0:T(1024)(128)(4,1)}), s8[4194304]{0:T(1024)(128)(4,1)S(1)}, s32[]{:S(2)}) async-start(s8[4718592]{0:T(1024)(128)(4,1)} %bitcast.4), calls=%async_computation.2 | async-start | bytes 8388608
  323.3 3.3 copy-start.2
  323.3 4.3 %slice-start.3 = ((s8[4718592]{0:T(1024)(128)(4,1)}), s8[524288]{0:T(1024)(128)(4,1)S(1)}, s32[]{:S(2)}) async-start(s8[4718592]{0:T(1024)(128)(4,1)} %bitcast.4), calls=%async_computation.3 | async-start | bytes 1048576
  326.6 4.3 %slice-start = ((s8[4718592]{0:T(1024)(128)(4,1)}), s8[4194304]{0:T(1024)(128)(4,1)S(1)}, s32[]{:S(2)}) async-start(s8[4718592]{0:T(1024)(128)(4,1)} %bitcast.2), calls=%async_computation | async-start | bytes 8388608
  327.6 3.5 %slice-start.1 = ((s8[4718592]{0:T(1024)(128)(4,1)}), s8[524288]{0:T(1024)(128)(4,1)S(1)}, s32[]{:S(2)}) async-start(s8[4718592]{0:T(1024)(128)(4,1)} %bitcast.2), calls=%async_computation.1 | async-start | bytes 1048576

commit v2 on v1

--- a/solution.py
+++ b/solution.py
@@ -121,7 +121,7 @@
 class Final:
     def __init__(self, sums, shapes, count, places):
         self.sums, self.shapes, self.count, self.places = sums, shapes, count, places
-        self.at, self.flips = (0,), [0]
+        self.at, self.flips = (0, 2), [0]
 
     @property
     def inputs(self):
@@ -138,13 +138,23 @@
 
     def build(self, ins, outs, scratch, _):
         put = lambda sources: self.places(sources, outs, bit_of(0))
-        return [place_copies(put, ins, scratch[2:], 0, scratch[0], scratch[1])]
+        sems, load_sems, *held = scratch
+        there, loads, here = place_parts(put, ins, held, 0, sems, load_sems)
+
+        def wait_all():
+            for c in here + there:
+                c.wait()
+
+        return [
+            (lambda: [c.start() for c in there + loads], lambda: [c.wait() for c in loads]),
+            (lambda: [c.start() for c in here], wait_all),
+        ]
 
     def receive(self, outs):
         self.results = list(outs)
 
 
-def place_copies(put, sources, held, flip, sems, load_sems):
+def place_parts(put, sources, held, flip, sems, load_sems):
     at = (lambda k, j: sems.at[k]) if load_sems is None else (lambda k, j: sems.at[k, j])
     there = [
         pltpu.make_async_remote_copy(
@@ -156,6 +166,11 @@
         pltpu.make_async_copy(s, h, sems.at[2] if load_sems is None else load_sems.at[j]) for j, (s, h) in enumerate(zip(sources, held))
     ]
     here = [pltpu.make_async_copy(s, t, at(2, j)) for j, (s, t) in enumerate(put(sources if held is None else held))]
+    return there, loads, here
+
+
+def place_copies(put, sources, held, flip, sems, load_sems):
+    there, loads, here = place_parts(put, sources, held, flip, sems, load_sems)
 
     def begin():
         for c in there + (here if held is None else loads):
@@ -403,9 +418,8 @@
 
 
 def gelu_pair(h):
-    a = jnp.abs(h) * np.float32(math.sqrt(0.5))
-    t = 1.0 / (1.0 + np.float32(0.3275911) * a)
-    bell = jnp.exp(-0.5 * (h * h))
+    t = 1.0 / (1.0 + np.float32(0.3275911 * math.sqrt(0.5)) * jnp.abs(h))
+    bell = jnp.exp2((h * h) * np.float32(-0.5 * math.log2(math.e)))
     poly = np.float32(0.5 * 1.061405429) * t + np.float32(0.5 * -1.453152027)
     poly = poly * t + np.float32(0.5 * 1.421413741)
     poly = poly * t + np.float32(0.5 * -0.284496736)
@@ -654,6 +668,7 @@
 
 
 VROWS = 80
+LOG2E = np.float32(math.log2(math.e))
 
 
 def forward_tile(q0, tq, tk, first, places, qt, k, vone, ot, qpad, acc):
@@ -675,7 +690,7 @@
             scores.append(jnp.where(allowed, s, -1e30))
         for h in range(heads):
             new.append(jnp.maximum(peaks[h], jnp.max(scores[h], axis=0, keepdims=True)))
-            raised.append(jnp.exp(scores[h] - new[h]).astype(bf16))
+            raised.append(jnp.exp2((scores[h] - new[h]) * LOG2E).astype(bf16))
         for h in range(heads):
             o = dot(vone[h, :, pl.ds(k0, tk)], raised[h])
             acc[h] = acc[h] * jnp.exp(peaks[h] - new[h]) + o
@@ -778,7 +793,7 @@
 
     if own:
         places = q0 + lax.broadcasted_iota(jnp.int32, (1, tq), 1)
-        forward_tile(q0, tq, tk, first_tokens(lens, places), places, qt, k, vone, ot, qpad, acc)
+        forward_tile(q0, tq, 2 * tk, first_tokens(lens, places), places, qt, k, vone, ot, qpad, acc)
         ot_send[...] = ot[...]
         low[:, pl.ds(q0, tq)] = ot[: ow.shape[0], :].astype(bf16)
     places = q0 + lax.broadcasted_iota(jnp.int32, (tq, 1), 0)
@@ -969,9 +984,10 @@
             at += rows
             if at == sizes[which]:
                 which, at = which + 1, 0
-    n = upb.shape[0]
+    n = upb.shape[1] // d
     bias_rows[...] = jnp.zeros_like(bias_rows)
-    bias_rows[:n, :] = upb[...].astype(f32)
+    for c in range(n):
+        bias_rows[c : c + 1, :] = upb[:, c * d : (c + 1) * d].astype(f32)
     for c in range(2):
         bias_rows[n : n + 1, c * e : (c + 1) * e] = qkvb[c : c + 1, :].astype(f32)
 
@@ -993,11 +1009,11 @@
         pack_kernel,
         grid=(1,),
         scalars=1,
-        in_specs=blocks(0) + blocks(1) + [whole((wide // d, d)), whole((2, e))],
+        in_specs=blocks(0) + blocks(1) + [whole((1, wide)), whole((2, e))],
         out_specs=[once((r, d)) for r in sizes],
         out_shape=[jax.ShapeDtypeStruct((r, d), f32) for r in sizes],
         name="pack",
-    )(meta, w, ow, up, down, w, ow, up, down, upb.reshape(-1, d), qkvb)
+    )(meta, w, ow, up, down, w, ow, up, down, upb[None], qkvb)
 
 
 def unpack(pieces, w, ow, up, down):

time: 334 us -> 332 us (level)
  no operation moved by 1% of the time
where the time goes in v2:
time: 332 us; the launch traced here: 331 us
  Pallas kernels  306 us (92%)
  local copies, waits for them, and re-layouts  22.9 us (7%)
    pallas_call x8, Pallas kernels, run(): pl.pallas_call(body, grid_spec=pltpu.PrefetchScalarGridSpec(num_scalar_pr...  306 us
    unnamed x29, local copies, waits for them, and re-layouts  16.2 us
  transfers between devices with their start and end apart: 1, of which 0 were waited for; matrix products, arithmetic and copies ran while one was open for 0% of the time, Pallas kernels for 24%

profile of v2, /device:TPU:0, one launch (start us, length us, event | category | flops | bytes accessed | tf_op | source)
XLA Modules:
  0.0 331.5 jit_solution(7739197064359479541)
XLA Ops:
  0.7 1.3 broadcast_in_dim.9.refs_9_
  1.9 0.6 pad_add_fusion.refs_0_
  2.5 5.1 %pack.1 = (f32[288,768]{1,0:T(8,128)}, f32[336,768]{1,0:T(8,128)}, f32[528,768]{1,0:T(8,128)}, f32[528,768]{1,0:T(8,128)}, f32[8,768]{1,0:T(8,128)}) custom-call(s32[2]{0:T(128)} %pad_add_fusion.refs_0_, bf16[3,768,384]{2,1,0:T(8,128)(2,1)} %refs_5_.7, bf16[384,768]{1,0:T(8,128)(2,1)} %refs_6_.8, bf16[768,1536]{1,0:T(8,128)(2,1)} %refs_2_.5, ...), custom_call_target="tpu_custom_call" | custom-call | tf_op jit(solution)/shard_map/pack/pallas_call | solution.py:378
  7.6 0.0 copy-start.6
  7.6 53.8 %mlp_own.1 = (f32[2048,768]{1,0:T(8,128)}, f32[2048,768]{1,0:T(8,128)}, f32[384,768]{1,0:T(8,128)}, f32[384,768]{1,0:T(8,128)}, f32[384,768]{1,0:T(8,128)}, /*in...) custom-call(bf16[2048,768]{1,0:T(8,128)(2,1)} %refs_0_.9, ...), custom_call_target="tpu_custom_call" | custom-call | flops 579820584960 | bytes 25165824 | tf_op jit(solution)/shard_map/mlp_own/pallas_call | solution.py:378
  61.4 0.0 copy-done.6
  61.4 0.7 jit_solution_.3.refs_8_
  62.1 84.7 %attention.2 = (f32[392,2048]{1,0:T(8,128)}, f32[392,2048]{1,0:T(8,128)}, bf16[384,2048]{1,0:T(8,128)(2,1)}, bf16[384,2048]{1,0:T(8,128)(2,1)}, bf16[384,2048]{1...) custom-call(s32[1,8]{1,0:T(1,128)} %refs_0_.8, ...), custom_call_target="tpu_custom_call" | custom-call | flops 257698037760 | bytes 15728640 | tf_op jit(solution)/shard_map/attention/pallas_call | solution.py:378
  146.8 1.6 collective-permute-start
  148.4 26.2 %merge_own.1 = (f32[2048,768]{1,0:T(8,128)}, f32[2048,768]{1,0:T(8,128)}, f32[288,768]{1,0:T(8,128)}, f32[288,768]{1,0:T(8,128)}, f32[288,768]{1,0:T(8,128)}, /*...) custom-call(bf16[2048,768]{1,0:T(8,128)(2,1)} %refs_0_.9, ...), custom_call_target="tpu_custom_call" | custom-call | flops 193273528320 | bytes 37748736 | tf_op jit(solution)/shard_map/merge_own/pallas_call | solution.py:378
  174.5 0.0 copy-start.4
  174.6 0.0 copy-start.5
  174.6 53.7 %mlp_other.1 = (f32[2048,768]{1,0:T(8,128)}, f32[2048,768]{1,0:T(8,128)}, bf16[3,768,384]{2,1,0:T(8,128)(2,1)}, bf16[384,768]{1,0:T(8,128)(2,1)}, f32[8,768]{1,0...) custom-call(f32[288,768]{1,0:T(8,128)} %get-tuple-element.97.refs_19, ...), custom_call_target="tpu_custom_call" | custom-call | flops 386547056640 | bytes 25165824 | tf_op jit(solution)/shard_map/mlp_other/pallas_call | solution.py:378
  228.3 0.0 copy-done.4
  228.3 0.6 broadcast_in_dim.10.refs_10_
  228.9 0.0 copy-done.5
  228.9 0.6 broadcast_in_dim.11.refs_11_
  229.5 0.0 collective-permute-done.refs_0_
  229.5 61.2 %attention.3 = (bf16[384,2048]{1,0:T(8,128)(2,1)}, bf16[384,2048]{1,0:T(8,128)(2,1)}, bf16[384,2048]{1,0:T(8,128)(2,1)}, f32[144,768]{1,0:T(8,128)}, f32[288,768...) custom-call(s32[1,8]{1,0:T(1,128)} %refs_0_.8, ...), custom_call_target="tpu_custom_call" | custom-call | flops 257698037760 | bytes 15728640 | tf_op jit(solution)/shard_map/attention/pallas_call | solution.py:378
  290.6 21.0 %merge_other.1 = (bf16[2048,768]{1,0:T(8,128)(2,1)}, bf16[2048,768]{1,0:T(8,128)(2,1)}, f32[8,768]{1,0:T(8,128)}, f32[1536,768]{1,0:T(8,128)}, f32[768,1536]{1,0...) custom-call(bf16[2048,768]{1,0:T(8,128)(2,1)} %refs_0_.9, bf16[2048,768]{1,0:T(8,128)(2,1)} %refs_1_.9, ...), custom_call_target="tpu_custom_call" | custom-call | flops 96636764160 | bytes 37748736 | tf_op jit(solution)/shard_map/merge_other/pallas_call | solution.py:378
  311.7 1.5 fusion
  313.1 0.0 copy-start.1
  313.1 0.9 slice_reduce_fusion
  314.1 0.0 copy-start.3
  314.1 0.6 slice.26
  314.7 0.6 reshape.31
  315.3 0.6 copy.35
  315.9 0.0 copy-start
  315.9 3.9 %copy.36 = bf16[2048,768]{1,0:T(8,128)(2,1)} copy(bf16[2048,768]{1,0:T(8,128)(2,1)} %get-tuple-element.217) | data formatting | bytes 6291456
  319.8 0.0 copy-done.3
  319.8 0.0 copy-done.1
  319.8 0.0 slice-start.2
  319.8 1.7 copy.37
  321.4 0.0 copy-done
  321.4 0.0 copy-start.2
  321.4 0.0 slice-start.3
  321.4 1.8 copy.38
  323.3 1.5 copy-done.2
  324.7 0.0 slice-start
  324.7 1.0 copy.39
  325.7 0.0 slice-done.2
  325.7 0.0 slice-done.3
  325.7 0.0 slice-start.1
  325.7 2.4 copy.40
  328.2 0.8 slice-done
  329.0 0.3 slice-done.1
  329.3 2.2 copy.41
  (3 shorter events, 0.0 us)
Async XLA Ops:
  7.6 53.8 %copy-start.6 = (f32[8]{0:T(128)S(1)}, f32[8]{0:T(128)}, u32[]{:S(2)}) copy-start(f32[8]{0:T(128)} %constant.12.clone) | copy-start | bytes 100
  146.8 82.6 %collective-permute-start = (f32[392,2048]{1,0:T(8,128)}, f32[392,2048]{1,0:T(8,128)}, u32[]{:S(2)}, u32[]{:S(2)}) collective-permute-start(f32[392,2048]{1,0:T(8,128)} %get-tuple-element.149), channel_id=1, source_target_pairs={{0,1},{1,0},{2,3},{3,2},{4,5},{5,4},{6,7},{7,6},{8,9},{9,8},{10,11... | collective-permute-start | bytes 9633800 | tf_op jit(solution)/shard_map/ppermute | solution.py:1059
  174.5 53.8 %copy-start.4 = (bf16[768]{0:T(1024)(128)(2,1)S(1)}, bf16[768]{0:T(1024)(128)(2,1)}, u32[]{:S(2)}) copy-start(bf16[768]{0:T(1024)(128)(2,1)} %param.19) | copy-start | bytes 4612
  174.6 54.3 %copy-start.5 = (bf16[768]{0:T(1024)(128)(2,1)S(1)}, bf16[768]{0:T(1024)(128)(2,1)}, u32[]{:S(2)}) copy-start(bf16[768]{0:T(1024)(128)(2,1)} %param.23) | copy-start | bytes 4612
  313.1 6.6 %copy-start.1 = (bf16[2048,768]{1,0:T(8,128)(2,1)S(1)}, bf16[2048,768]{1,0:T(8,128)(2,1)}, u32[]{:S(2)}) copy-start(bf16[2048,768]{1,0:T(8,128)(2,1)} %get-tuple-element.218) | copy-start | bytes 9437188
  314.1 5.7 %copy-start.3 = (f32[768]{0:T(1024)}, f32[768]{0:T(1024)S(1)}, u32[]{:S(2)}) copy-start(f32[768]{0:T(1024)S(1)} %get-tuple-element.222) | copy-start | bytes 9220
  315.9 5.6 %copy-start = (f32[3,768,384]{2,1,0:T(8,128)S(1)}, f32[3,768,384]{2,1,0:T(8,128)}, u32[]{:S(2)}) copy-start(f32[3,768,384]{2,1,0:T(8,128)} %get-tuple-element.219) | copy-start | bytes 10616836
  319.8 6.0 %slice-start.2 = ((s8[4718592]{0:T(1024)(128)(4,1)}), s8[4194304]{0:T(1024)(128)(4,1)S(1)}, s32[]{:S(2)}) async-start(s8[4718592]{0:T(1024)(128)(4,1)} %bitcast.4), calls=%async_computation.2 | async-start | bytes 8388608
  321.4 3.3 copy-start.2
  321.4 4.3 %slice-start.3 = ((s8[4718592]{0:T(1024)(128)(4,1)}), s8[524288]{0:T(1024)(128)(4,1)S(1)}, s32[]{:S(2)}) async-start(s8[4718592]{0:T(1024)(128)(4,1)} %bitcast.4), calls=%async_computation.3 | async-start | bytes 1048576
  324.7 4.3 %slice-start = ((s8[4718592]{0:T(1024)(128)(4,1)}), s8[4194304]{0:T(1024)(128)(4,1)S(1)}, s32[]{:S(2)}) async-start(s8[4718592]{0:T(1024)(128)(4,1)} %bitcast.2), calls=%async_computation | async-start | bytes 8388608
  325.7 3.5 %slice-start.1 = ((s8[4718592]{0:T(1024)(128)(4,1)}), s8[524288]{0:T(1024)(128)(4,1)S(1)}, s32[]{:S(2)}) async-start(s8[4718592]{0:T(1024)(128)(4,1)} %bitcast.2), calls=%async_computation.1 | async-start | bytes 1048576

commit v3 on v2

--- a/solution.py
+++ b/solution.py
@@ -759,7 +759,7 @@
     refs = list(refs)
     cut = lambda n: [refs.pop(0) for _ in range(n)]
     if own:
-        ot, ot_send, grads_q, grads_k, grads_v, keep_o, send_o = cut(7)
+        ot, grads_q, grads_k, grads_v, keep_o, send_o = cut(6)
     else:
         ot, grads_q, grads_k, grads_v = cut(4)
     q, qt, k, kpad, vpad, do, dot_t, cosine, sine, dk, dv, dq, qa, da, cs, cd = cut(16)
@@ -791,15 +791,28 @@
 
         lax.fori_loop(0, length // tile, some, 0)
 
+    @pl.when(q0 < FILLED)
+    def _():
+        if own:
+            places = q0 + lax.broadcasted_iota(jnp.int32, (1, tq), 1)
+            forward_tile(q0, tq, 2 * tk, first_tokens(lens, places), places, qt, k, vone, ot, qpad, acc)
+        places = q0 + lax.broadcasted_iota(jnp.int32, (tq, 1), 0)
+        backward_tile(
+            q0, tq, tk, first_tokens(lens, places), places, q, qt, k, kpad, vpad, do, dot_t, ot, cosine, sine, grads_q, dk, dv, dq, qa, da, cs, cd
+        )
+
+    @pl.when(q0 >= FILLED)
+    def _():
+        cols = pl.ds(q0, tq)
+        if own:
+            for h in range(heads):
+                ot[h * HEAD : (h + 1) * HEAD, :] = vone[h, :HEAD, cols].astype(f32)
+            ot[heads * HEAD :, :] = jnp.zeros((8, tq), f32)
+        grads_q[...] = jnp.zeros_like(grads_q)
+        dv[:, cols] = dot_t[:, cols].astype(f32)
+
     if own:
-        places = q0 + lax.broadcasted_iota(jnp.int32, (1, tq), 1)
-        forward_tile(q0, tq, 2 * tk, first_tokens(lens, places), places, qt, k, vone, ot, qpad, acc)
-        ot_send[...] = ot[...]
         low[:, pl.ds(q0, tq)] = ot[: ow.shape[0], :].astype(bf16)
-    places = q0 + lax.broadcasted_iota(jnp.int32, (tq, 1), 0)
-    backward_tile(
-        q0, tq, tk, first_tokens(lens, places), places, q, qt, k, kpad, vpad, do, dot_t, ot, cosine, sine, grads_q, dk, dv, dq, qa, da, cs, cd
-    )
 
     @pl.when(i == pl.num_programs(0) - 1)
     def _():
@@ -836,8 +849,8 @@
         in_specs=[
             *[pl.BlockSpec(memory_space=pl.ANY)] * 2, whole((3, d, e)), whole((8, d)), whole((e, d)), whole((2, d)), whole((2, d)), whole((HALF, 128)),
         ] + ([] if own else [stat]),
-        out_specs=([stat, stat] if own else []) + [cols, whole((e, length)), whole((e, length))] + ([whole(half.shape)] * 2 if own else []),
-        out_shape=([kept, kept] if own else []) + [grad, grad, grad] + ([half, half] if own else []),
+        out_specs=([stat] if own else []) + [cols, whole((e, length)), whole((e, length))] + ([whole(half.shape)] * 2 if own else []),
+        out_shape=([kept] if own else []) + [grad, grad, grad] + ([half, half] if own else []),
         scratch=scratch,
         flops=8 * length * length * e,
         nbytes=20 * length * e,
@@ -1153,13 +1166,13 @@
     down_2, up_2 = Sum(keep_d, send_d, order), Sum(keep_u, send_u, crossed)
     send = Sends((three, "tensor"), (far_three, "tensor"), (one, 0), (two, 0))
     near = [Sends((one, 1), at=(2,)), Sends((two, 1), at=(5,))]
-    ot, ot_send, gq, gk, gv, keep_o, send_o = attention(
+    ot, gq, gk, gv, keep_o, send_o = attention(
         wide // d, lengths, tokens, cotangent, qkv_weight, own_biases, out_weight, norm_gains, norm_biases, freq,
         rides=[down_1.take(0, 1, 4), up_1.take(0, 1, 4), down_2.take(0, 1, 5, 6), up_2.take(0, 1, 5, 6), send] + near, collective=2,
     )
     three, near_three, core_one, core_two = send.got
     (near_one,), (near_two,) = near[0].got, near[1].got
-    other_ot = across(ot_send)
+    other_ot = across(ot)
     sum_o = Sum(keep_o, send_o, order, True)
     send = Sends((near_one, 0), (near_two, 0), (near_three, 0), (three, 0))
     part, share, keep_a, send_a, keep_b, send_b, small = merge_own(

time: 332 us -> 332 us (level)
  no operation moved by 1% of the time
where the time goes in v3:
time: 332 us
  Pallas kernels  306 us (92%)
  local copies, waits for them, and re-layouts  23 us (7%)
    pallas_call x8, Pallas kernels, run(): pl.pallas_call(body, grid_spec=pltpu.PrefetchScalarGridSpec(num_scalar_pr...  306 us
    unnamed x29, local copies, waits for them, and re-layouts  16.4 us
  transfers between devices with their start and end apart: 1, of which 0 were waited for; matrix products, arithmetic and copies ran while one was open for 0% of the time, Pallas kernels for 24%

profile of v3, /device:TPU:0, one launch (start us, length us, event | category | flops | bytes accessed | tf_op | source)
XLA Modules:
  0.0 331.5 jit_solution(17747181505186930179)
XLA Ops:
  0.7 1.3 broadcast_in_dim.9.refs_9_
  1.9 0.6 pad_add_fusion.refs_0_
  2.5 5.1 %pack.1 = (f32[288,768]{1,0:T(8,128)}, f32[336,768]{1,0:T(8,128)}, f32[528,768]{1,0:T(8,128)}, f32[528,768]{1,0:T(8,128)}, f32[8,768]{1,0:T(8,128)}) custom-call(s32[2]{0:T(128)} %pad_add_fusion.refs_0_, bf16[3,768,384]{2,1,0:T(8,128)(2,1)} %refs_5_.7, bf16[384,768]{1,0:T(8,128)(2,1)} %refs_6_.8, bf16[768,1536]{1,0:T(8,128)(2,1)} %refs_2_.5, ...), custom_call_target="tpu_custom_call" | custom-call | tf_op jit(solution)/shard_map/pack/pallas_call | solution.py:378
  7.6 0.0 copy-start.6
  7.6 53.7 %mlp_own.1 = (f32[2048,768]{1,0:T(8,128)}, f32[2048,768]{1,0:T(8,128)}, f32[384,768]{1,0:T(8,128)}, f32[384,768]{1,0:T(8,128)}, f32[384,768]{1,0:T(8,128)}, /*in...) custom-call(bf16[2048,768]{1,0:T(8,128)(2,1)} %refs_0_.9, ...), custom_call_target="tpu_custom_call" | custom-call | flops 579820584960 | bytes 25165824 | tf_op jit(solution)/shard_map/mlp_own/pallas_call | solution.py:378
  61.3 0.0 copy-done.6
  61.3 0.7 jit_solution_.3.refs_8_
  62.0 84.7 %attention.2 = (f32[392,2048]{1,0:T(8,128)}, bf16[384,2048]{1,0:T(8,128)(2,1)}, bf16[384,2048]{1,0:T(8,128)(2,1)}, bf16[384,2048]{1,0:T(8,128)(2,1)}, f32[192,76...) custom-call(s32[1,8]{1,0:T(1,128)} %refs_0_.8, ...), custom_call_target="tpu_custom_call" | custom-call | flops 257698037760 | bytes 15728640 | tf_op jit(solution)/shard_map/attention/pallas_call | solution.py:378
  146.7 1.6 collective-permute-start
  148.2 26.0 %merge_own.1 = (f32[2048,768]{1,0:T(8,128)}, f32[2048,768]{1,0:T(8,128)}, f32[288,768]{1,0:T(8,128)}, f32[288,768]{1,0:T(8,128)}, f32[288,768]{1,0:T(8,128)}, /*...) custom-call(bf16[2048,768]{1,0:T(8,128)(2,1)} %refs_0_.9, ...), custom_call_target="tpu_custom_call" | custom-call | flops 193273528320 | bytes 37748736 | tf_op jit(solution)/shard_map/merge_own/pallas_call | solution.py:378
  174.2 0.0 copy-start.4
  174.2 0.0 copy-start.5
  174.3 53.8 %mlp_other.1 = (f32[2048,768]{1,0:T(8,128)}, f32[2048,768]{1,0:T(8,128)}, bf16[3,768,384]{2,1,0:T(8,128)(2,1)}, bf16[384,768]{1,0:T(8,128)(2,1)}, f32[8,768]{1,0...) custom-call(f32[288,768]{1,0:T(8,128)} %get-tuple-element.96.refs_19, ...), custom_call_target="tpu_custom_call" | custom-call | flops 386547056640 | bytes 25165824 | tf_op jit(solution)/shard_map/mlp_other/pallas_call | solution.py:378
  228.1 0.0 copy-done.4
  228.1 0.6 broadcast_in_dim.10.refs_10_
  228.7 0.0 copy-done.5
  228.7 0.6 broadcast_in_dim.11.refs_11_
  229.2 0.0 collective-permute-done.refs_0_
  229.2 61.3 %attention.3 = (bf16[384,2048]{1,0:T(8,128)(2,1)}, bf16[384,2048]{1,0:T(8,128)(2,1)}, bf16[384,2048]{1,0:T(8,128)(2,1)}, f32[144,768]{1,0:T(8,128)}, f32[288,768...) custom-call(s32[1,8]{1,0:T(1,128)} %refs_0_.8, ...), custom_call_target="tpu_custom_call" | custom-call | flops 257698037760 | bytes 15728640 | tf_op jit(solution)/shard_map/attention/pallas_call | solution.py:378
  290.5 21.1 %merge_other.1 = (bf16[2048,768]{1,0:T(8,128)(2,1)}, bf16[2048,768]{1,0:T(8,128)(2,1)}, f32[8,768]{1,0:T(8,128)}, f32[1536,768]{1,0:T(8,128)}, f32[768,1536]{1,0...) custom-call(bf16[2048,768]{1,0:T(8,128)(2,1)} %refs_0_.9, bf16[2048,768]{1,0:T(8,128)(2,1)} %refs_1_.9, ...), custom_call_target="tpu_custom_call" | custom-call | flops 96636764160 | bytes 37748736 | tf_op jit(solution)/shard_map/merge_other/pallas_call | solution.py:378
  311.7 0.8 slice_reduce_fusion
  312.5 0.0 copy-start.3
  312.5 1.5 fusion
  314.0 0.6 reshape.31
  314.6 0.6 slice.26
  315.2 0.0 copy-start.1
  315.2 0.6 copy.35
  315.8 0.0 copy-start
  315.8 4.0 %copy.36 = bf16[2048,768]{1,0:T(8,128)(2,1)} copy(bf16[2048,768]{1,0:T(8,128)(2,1)} %get-tuple-element.215) | data formatting | bytes 6291456
  319.8 0.0 copy-done.3
  319.8 0.0 copy-done.1
  319.8 0.0 slice-start.2
  319.8 1.7 copy.37
  321.5 0.0 copy-done
  321.5 0.0 copy-start.2
  321.5 0.0 slice-start.3
  321.5 1.8 copy.38
  323.3 1.5 copy-done.2
  324.8 0.0 slice-start
  324.8 1.0 copy.39
  325.8 0.0 slice-done.2
  325.8 0.0 slice-done.3
  325.8 0.0 slice-start.1
  325.8 2.4 copy.40
  328.2 0.8 slice-done
  329.0 0.3 slice-done.1
  329.3 2.2 copy.41
  (3 shorter events, 0.0 us)
Async XLA Ops:
  7.6 53.7 %copy-start.6 = (f32[8]{0:T(128)S(1)}, f32[8]{0:T(128)}, u32[]{:S(2)}) copy-start(f32[8]{0:T(128)} %constant.12.clone) | copy-start | bytes 100
  146.7 82.6 %collective-permute-start = (f32[392,2048]{1,0:T(8,128)}, f32[392,2048]{1,0:T(8,128)}, u32[]{:S(2)}, u32[]{:S(2)}) collective-permute-start(f32[392,2048]{1,0:T(8,128)} %get-tuple-element.117.refs_4_), channel_id=1, source_target_pairs={{0,1},{1,0},{2,3},{3,2},{4,5},{5,4},{6,7},{7,6},{8,9},{9,8},{10,11... | collective-permute-start | bytes 9633800 | tf_op jit(solution)/shard_map/ppermute | solution.py:1072
  174.2 53.8 %copy-start.4 = (bf16[768]{0:T(1024)(128)(2,1)S(1)}, bf16[768]{0:T(1024)(128)(2,1)}, u32[]{:S(2)}) copy-start(bf16[768]{0:T(1024)(128)(2,1)} %param.19) | copy-start | bytes 4612
  174.2 54.4 %copy-start.5 = (bf16[768]{0:T(1024)(128)(2,1)S(1)}, bf16[768]{0:T(1024)(128)(2,1)}, u32[]{:S(2)}) copy-start(bf16[768]{0:T(1024)(128)(2,1)} %param.23) | copy-start | bytes 4612
  312.5 7.3 %copy-start.3 = (f32[768]{0:T(1024)}, f32[768]{0:T(1024)S(1)}, u32[]{:S(2)}) copy-start(f32[768]{0:T(1024)S(1)} %get-tuple-element.220) | copy-start | bytes 9220
  315.2 4.7 %copy-start.1 = (bf16[2048,768]{1,0:T(8,128)(2,1)S(1)}, bf16[2048,768]{1,0:T(8,128)(2,1)}, u32[]{:S(2)}) copy-start(bf16[2048,768]{1,0:T(8,128)(2,1)} %get-tuple-element.216) | copy-start | bytes 9437188
  315.8 5.7 %copy-start = (f32[3,768,384]{2,1,0:T(8,128)S(1)}, f32[3,768,384]{2,1,0:T(8,128)}, u32[]{:S(2)}) copy-start(f32[3,768,384]{2,1,0:T(8,128)} %get-tuple-element.217) | copy-start | bytes 10616836
  319.8 6.0 %slice-start.2 = ((s8[4718592]{0:T(1024)(128)(4,1)}), s8[4194304]{0:T(1024)(128)(4,1)S(1)}, s32[]{:S(2)}) async-start(s8[4718592]{0:T(1024)(128)(4,1)} %bitcast.4), calls=%async_computation.2 | async-start | bytes 8388608
  321.5 3.3 copy-start.2
  321.5 4.3 %slice-start.3 = ((s8[4718592]{0:T(1024)(128)(4,1)}), s8[524288]{0:T(1024)(128)(4,1)S(1)}, s32[]{:S(2)}) async-start(s8[4718592]{0:T(1024)(128)(4,1)} %bitcast.4), calls=%async_computation.3 | async-start | bytes 1048576
  324.8 4.3 %slice-start = ((s8[4718592]{0:T(1024)(128)(4,1)}), s8[4194304]{0:T(1024)(128)(4,1)S(1)}, s32[]{:S(2)}) async-start(s8[4718592]{0:T(1024)(128)(4,1)} %bitcast.2), calls=%async_computation | async-start | bytes 8388608
  325.8 3.5 %slice-start.1 = ((s8[4718592]{0:T(1024)(128)(4,1)}), s8[524288]{0:T(1024)(128)(4,1)S(1)}, s32[]{:S(2)}) async-start(s8[4718592]{0:T(1024)(128)(4,1)} %bitcast.2), calls=%async_computation.1 | async-start | bytes 1048576
